TPU v7x, 512 devices: a whole 4x8x8 slice. The times are simulated.
512 devices in a mesh: gx: 8 (over z), gy: 8 (over y_lo, core), gz: 8 (over x, y_hi).
Axes of the slice: x: 4, y: 8 (y_hi: 2, y_lo: 4; y = y_hi * 4 + y_lo), z: 8, core: 2. Of those that a mesh axis runs over, the one named last changes fastest.
Arguments:
- node_irreps: bfloat16 [8, 8, 8, 16, 25, 128], P('gx', 'gy', 'gz'), may hold values from -5 to 11
- positions: float32 [8, 8, 8, 3, 16], P('gx', 'gy', 'gz'), may hold values from 0 to 6.8
- send_list: int32 [8, 8, 8, 8], P('gx', 'gy', 'gz'), may hold values from 0 to 15, as said below
- neighbours: int32 [8, 8, 8, 16, 32], P('gx', 'gy', 'gz'), may hold values from 0 to 231
- displacements: float32 [8, 8, 8, 3, 512], P('gx', 'gy', 'gz'), may hold values from -6 to 6
- order_zero: bfloat16 [640, 640], replicated, may hold values from -0.25 to 0.25
- order_one: bfloat16 [512, 1024], replicated, may hold values from -0.25 to 0.25
- order_two: bfloat16 [384, 768], replicated, may hold values from -0.3125 to 0.3125
- reciprocal_triples: int32 [1024, 3], replicated, may hold values from -6 to 6
- reciprocal_filter: float32 [1024, 128], replicated, may hold values from 0.1 to 1
- cotangent: float32 [8, 8, 8, 16, 128], P('gx', 'gy', 'gz'), may hold values from -5 to 11
Outputs:
- updated: bfloat16 [8, 8, 8, 16, 25, 128], P('gx', 'gy', 'gz')
- long_range: float32 [8, 8, 8, 16, 128], P('gx', 'gy', 'gz')
- charge_grad: float32 [8, 8, 8, 16, 128], P('gx', 'gy', 'gz')
- position_grad: float32 [8, 8, 8, 3, 16], P('gx', 'gy', 'gz')
Inputs may be any that keep to these rules, and one draw needn't show every extreme that they name: `send_list`: entries of one block are distinct atoms of that block.
All inputs are finite; a program needn't handle non-finite values.
Results may differ from a plain program's by a relative error of at most 0.0023.
Values may be sent and summed in bfloat16 or wider, within the bound.
A program may use at most 64 MiB of HBM per device.

v0:
```python
import math

import jax
import jax.numpy as jnp
from jax import lax
from jax.sharding import PartitionSpec as P

highest = lax.Precision.HIGHEST
cell_length = 6.8
planar_floor = 0.25
radial_width = 64.0


def with_halo(block, sides, width):
    for axis, dim in sides:
        count = lax.axis_size(axis)
        forward = [(i, i + 1) for i in range(count - 1)]
        forward.append((count - 1, 0))
        backward = [(target, source) for source, target in forward]
        low = lax.ppermute(
            lax.slice_in_dim(block, block.shape[dim] - width, None, axis=dim), axis, forward
        )
        high = lax.ppermute(lax.slice_in_dim(block, 0, width, axis=dim), axis, backward)
        block = jnp.concatenate([low, block, high], axis=dim)
    return block


def harmonic_slot(degree, signed_order):
    return degree * degree + degree + signed_order


def kept_rows():
    layout = []
    for degree in range(5):
        for signed_order in range(-degree, degree + 1):
            layout.append(harmonic_slot(degree, signed_order))
    return layout


def edge_messages(
    lookup_table, displacement, neighbour_index, order_zero, order_one, order_two, layout
):
    atom_count = neighbour_index.shape[0]
    neighbour_count = neighbour_index.shape[1]
    flat_index = neighbour_index.reshape(-1)
    edge_count = flat_index.shape[0]
    feature_width = lookup_table.shape[2]
    source = lookup_table[flat_index]
    length_squared = jnp.sum(displacement * displacement, axis=0)
    radial = jnp.exp(-length_squared / radial_width) / math.sqrt(neighbour_count)
    planar = jnp.sqrt(
        displacement[0] * displacement[0] + displacement[1] * displacement[1] + planar_floor
    )
    cos_one = displacement[0] / planar
    sin_one = displacement[1] / planar

    def neighbour_sum(values):
        weighted = values * radial[:, None, None]
        return jnp.sum(
            weighted.reshape(atom_count, neighbour_count, values.shape[1], feature_width), axis=1
        )

    collected = {}
    zero_slots = [layout.index(harmonic_slot(degree, 0)) for degree in range(5)]
    zero_input = source[:, zero_slots, :].reshape(edge_count, 5 * feature_width)
    zero_output = jnp.dot(zero_input, order_zero, preferred_element_type=jnp.float32)
    summed_zero_part = neighbour_sum(zero_output.reshape(edge_count, 5, feature_width))
    for degree in range(5):
        collected[harmonic_slot(degree, 0)] = summed_zero_part[:, degree]
    rotations = (
        (1, cos_one, sin_one, order_one),
        (2, cos_one * cos_one - sin_one * sin_one, 2.0 * cos_one * sin_one, order_two),
    )
    for harmonic_order, cosine, sine_term, weight_pair in rotations:
        degrees = list(range(harmonic_order, 5))
        count_of_rows = len(degrees)
        plus_slots = [layout.index(harmonic_slot(degree, harmonic_order)) for degree in degrees]
        minus_slots = [layout.index(harmonic_slot(degree, -harmonic_order)) for degree in degrees]
        plus_part = source[:, plus_slots, :].astype(jnp.float32)
        minus_part = source[:, minus_slots, :].astype(jnp.float32)
        cosine_wide = cosine[:, None, None]
        sine_wide = sine_term[:, None, None]
        turned_plus = (cosine_wide * plus_part + sine_wide * minus_part).astype(jnp.bfloat16)
        turned_minus = (cosine_wide * minus_part - sine_wide * plus_part).astype(jnp.bfloat16)
        split_at = count_of_rows * feature_width
        stacked = jnp.concatenate(
            [turned_plus.reshape(edge_count, split_at), turned_minus.reshape(edge_count, split_at)],
            axis=0,
        )
        product = jnp.dot(stacked, weight_pair, preferred_element_type=jnp.float32)
        upper_half = product[:edge_count]
        lower_half = product[edge_count:]
        mixed_plus = (upper_half[:, :split_at] - lower_half[:, split_at:]).reshape(
            edge_count, count_of_rows, feature_width
        )
        mixed_minus = (upper_half[:, split_at:] + lower_half[:, :split_at]).reshape(
            edge_count, count_of_rows, feature_width
        )
        back_plus = neighbour_sum(cosine_wide * mixed_plus - sine_wide * mixed_minus)
        back_minus = neighbour_sum(sine_wide * mixed_plus + cosine_wide * mixed_minus)
        for position_in, degree in enumerate(degrees):
            collected[harmonic_slot(degree, harmonic_order)] = back_plus[:, position_in]
            collected[harmonic_slot(degree, -harmonic_order)] = back_minus[:, position_in]
    zero_block = jnp.zeros((atom_count, feature_width), jnp.float32)
    return jnp.stack([collected.get(slot_number, zero_block) for slot_number in range(25)], axis=1)


def table_product(table, values):
    return jnp.dot(table.T, values, precision=highest)


def local(
    node_irreps,
    positions,
    send_list,
    neighbours,
    displacements,
    order_zero,
    order_one,
    order_two,
    reciprocal_triples,
    reciprocal_filter,
    cotangent,
):
    local_irreps = node_irreps[0, 0, 0]
    atom_count = local_irreps.shape[0]
    size_x = lax.axis_size("gx")
    size_y = lax.axis_size("gy")
    size_z = lax.axis_size("gz")
    total_atom_count = atom_count * size_x * size_y * size_z
    scale_factor = 1.0 / math.sqrt(total_atom_count * reciprocal_filter.shape[0])
    corner = jnp.stack([lax.axis_index("gx"), lax.axis_index("gy"), lax.axis_index("gz")]).astype(
        jnp.float32
    )
    box = cell_length * jnp.array([size_x, size_y, size_z], jnp.float32)
    fractional = (positions[0, 0, 0] + cell_length * corner[:, None]) / box[:, None]
    wave_float = reciprocal_triples.astype(jnp.float32)
    phase = 2.0 * math.pi * jnp.dot(fractional.T, wave_float.T, precision=highest)
    cos_table = jnp.cos(phase)
    sin_table = jnp.sin(phase)
    charges = local_irreps[:, 0, :].astype(jnp.float32)
    grad_input = cotangent[0, 0, 0]
    raw_cos, raw_sin, charge_total, plane_cos, plane_sin = lax.psum(
        (
            table_product(cos_table, charges),
            table_product(sin_table, charges),
            jnp.sum(charges, axis=0),
            jnp.sum(cos_table, axis=0),
            jnp.sum(sin_table, axis=0),
        ),
        ("gx", "gy", "gz"),
    )
    resp_cos, resp_sin = lax.psum(
        (table_product(cos_table, grad_input), table_product(sin_table, grad_input)),
        ("gx", "gy", "gz"),
    )
    mean_charge = charge_total / total_atom_count
    centered = charges - mean_charge
    struct_cos = raw_cos - plane_cos[:, None] * mean_charge[None, :]
    struct_sin = raw_sin - plane_sin[:, None] * mean_charge[None, :]
    sent_rows = send_list[0, 0, 0]
    layout = kept_rows()
    arrived = with_halo(
        local_irreps[sent_rows][None, None, None], (("gx", 0), ("gy", 1), ("gz", 2)), 1
    )
    ghost_table = arrived.reshape((-1,) + local_irreps.shape[1:])
    lookup_table = jnp.concatenate([local_irreps, ghost_table], axis=0)
    messages = edge_messages(
        lookup_table,
        displacements[0, 0, 0],
        neighbours[0, 0, 0],
        order_zero,
        order_one,
        order_two,
        layout,
    )
    updated = (local_irreps.astype(jnp.float32) + messages).astype(jnp.bfloat16)
    long_range = scale_factor * (
        jnp.dot(cos_table, reciprocal_filter * struct_cos, precision=highest)
        + jnp.dot(sin_table, reciprocal_filter * struct_sin, precision=highest)
    )
    charge_term = scale_factor * (
        jnp.dot(cos_table, reciprocal_filter * resp_cos, precision=highest)
        + jnp.dot(sin_table, reciprocal_filter * resp_sin, precision=highest)
    )
    term_mean = (
        scale_factor
        * (
            jnp.dot(plane_cos, reciprocal_filter * resp_cos, precision=highest)
            + jnp.dot(plane_sin, reciprocal_filter * resp_sin, precision=highest)
        )
        / total_atom_count
    )
    charge_grad = charge_term - term_mean
    with_sin = jnp.dot(grad_input, (reciprocal_filter * struct_sin).T, precision=highest) + jnp.dot(
        centered, (reciprocal_filter * resp_sin).T, precision=highest
    )
    with_cos = jnp.dot(grad_input, (reciprocal_filter * struct_cos).T, precision=highest) + jnp.dot(
        centered, (reciprocal_filter * resp_cos).T, precision=highest
    )
    phase_grad = scale_factor * (cos_table * with_sin - sin_table * with_cos)
    position_grad = (2.0 * math.pi * jnp.dot(phase_grad, wave_float, precision=highest) / box).T
    return (
        updated[None, None, None],
        long_range[None, None, None],
        charge_grad[None, None, None],
        position_grad[None, None, None],
    )


def solution(mesh):
    return jax.shard_map(
        local,
        mesh=mesh,
        in_specs=(
            P("gx", "gy", "gz", None, None, None),
            P("gx", "gy", "gz", None, None),
            P("gx", "gy", "gz", None),
            P("gx", "gy", "gz", None, None),
            P("gx", "gy", "gz", None, None),
            P(),
            P(),
            P(),
            P(),
            P(),
            P("gx", "gy", "gz", None, None),
        ),
        out_specs=(
            P("gx", "gy", "gz", None, None, None),
            P("gx", "gy", "gz", None, None),
            P("gx", "gy", "gz", None, None),
            P("gx", "gy", "gz", None, None),
        ),
        check_vma=False,
    )
```

profile of v0, /device:TPU:1, one launch (start us, length us, event | category | flops | bytes accessed | tf_op | source)
XLA Modules:
  0.0 338.6 jit_solution(16953265022681854199)
XLA Ops:
  9.5 11.5 %collective-permute-start.1 = (bf16[1,1,1,8,25,128]{5,4,3,2,1,0:T(8,128)(2,1)S(1)}, bf16[1,1,1,8,25,128]{5,4,3,2,1,0:T(8,128)(2,1)S(1)}, u32[]{:S(2)}, u32[]{:S(2)}) collective-permute-start(bf16[1,1,1,8,25,128]{5,4,3,2,1,0:T(8,128)(2,1)S(1)} %bitcast.173), channel_id=1, source_target_pairs={{64,0},{128,64},{192,128},{256,192},{320,256},{384,320},{448,384},... | collective-permute-start | bytes 153608 | tf_op jit(solution)/shard_map/ppermute | solution.py:23
  21.0 1.9 collective-permute-start
  24.3 1.4 fusion.39
  25.7 1.4 fusion.41
  27.1 2.5 fusion.33
  29.7 1.8 fusion.35
  31.8 100.4 %all-reduce = (f32[128]{0:T(128)S(1)}, f32[1024]{0:T(1024)S(1)}, f32[1024]{0:T(1024)S(1)}) all-reduce(f32[128]{0:T(128)S(1)} %get-tuple-element.33, f32[1024]{0:T(1024)S(1)} %reduce_sum.87, f32[1024]{0:T(1024)S(1)} %reduce_sum.89), channel_id=1, replica_groups=mesh['gx'=8,'gy'=8,'gz'=8] {'gx','gy','gz'}, use_global_device_ids=true, to_apply=%region_10.0 | all-reduce | flops 2176 | bytes 17408 | tf_op jit(solution)/shard_map/psum | solution.py:143
  132.2 2.6 collective-permute-start.3
  134.8 2.9 collective-permute-start.2
  139.2 2.4 collective-permute-done.2
  141.9 4.4 %collective-permute-start.5 = (bf16[3,3,1,8,25,128]{5,3,4,2,1,0:T(8,128)(2,1)S(1)}, bf16[3,3,1,8,25,128]{5,3,4,2,1,0:T(8,128)(2,1)}, u32[]{:S(2)}, u32[]{:S(2)}) collective-permute-start(bf16[3,3,1,8,25,128]{5,3,4,2,1,0:T(8,128)(2,1)S(1)} %copy.50), channel_id=1, source_target_pairs={{1,0},{2,1},{3,2},{4,3},{5,4},{6,5},{7,6},{0,7},{9,8},{10,9},{11,1... | collective-permute-start | bytes 1382408 | tf_op jit(solution)/shard_map/ppermute | solution.py:23
  146.3 5.0 %collective-permute-start.4 = (bf16[3,3,1,8,25,128]{5,3,4,2,1,0:T(8,128)(2,1)S(1)}, bf16[3,3,1,8,25,128]{5,3,4,2,1,0:T(8,128)(2,1)}, u32[]{:S(2)}, u32[]{:S(2)}) collective-permute-start(bf16[3,3,1,8,25,128]{5,3,4,2,1,0:T(8,128)(2,1)S(1)} %copy.50), channel_id=1, source_target_pairs={{0,1},{1,2},{2,3},{3,4},{4,5},{5,6},{6,7},{7,0},{8,9},{9,10},{10,1... | collective-permute-start | bytes 1382408 | tf_op jit(solution)/shard_map/ppermute | solution.py:20
  154.2 5.0 %collective-permute-done.5 = bf16[3,3,1,8,25,128]{5,3,4,2,1,0:T(8,128)(2,1)} collective-permute-done((bf16[3,3,1,8,25,128]{5,3,4,2,1,0:T(8,128)(2,1)S(1)}, bf16[3,3,1,8,25,128]{5,3,4,2,1,0:T(8,128)(2,1)}, u32[]{:S(2)}, u32[]{:S(2)}) %collective-permute-start.5) | collective-permute-done | bytes 460832 | tf_op jit(solution)/shard_map/ppermute | solution.py:23
  160.3 9.0 %collective-permute-done.4 = bf16[3,3,1,8,25,128]{5,3,4,2,1,0:T(8,128)(2,1)} collective-permute-done((bf16[3,3,1,8,25,128]{5,3,4,2,1,0:T(8,128)(2,1)S(1)}, bf16[3,3,1,8,25,128]{5,3,4,2,1,0:T(8,128)(2,1)}, u32[]{:S(2)}, u32[]{:S(2)}) %collective-permute-start.4) | collective-permute-done | bytes 460832 | tf_op jit(solution)/shard_map/ppermute | solution.py:20
  171.0 3.5 %gather_fusion.1 = bf16[512,25,128]{2,1,0:T(8,128)(2,1)} fusion(bf16[232,25,128]{2,1,0:T(8,128)(2,1)S(1)} %pad_maximum_fusion, s32[1024]{0:T(1024)S(1)} %get-tuple-element.75), kind=kCustom, calls=%fused_computation.1 | custom fusion | bytes 6555648 | tf_op jit(solution)/shard_map/gather | solution.py:48
  174.5 5.2 %copy.56 = bf16[512,25,128]{2,0,1:T(8,128)(2,1)} copy(bf16[512,25,128]{2,1,0:T(8,128)(2,1)} %gather_fusion.1) | data formatting | bytes 6553600 | tf_op jit(solution)/shard_map/gather | solution.py:48
  179.7 3.3 gather_fusion.6
  183.0 2.5 gather_fusion.5
  188.1 3.4 gather_fusion.4
  191.4 3.4 gather_fusion.3
  194.8 2.6 gather_fusion.2
  198.5 2.2 bitcast_reduce_fusion
  204.6 1.4 fusion.25
  208.4 1.4 reshape.294
  209.9 3.1 multiply_reduce_fusion
  214.7 1.8 slice_subtract_fusion
  216.5 1.6 reshape.291
  218.1 2.6 reshape.292
  220.7 3.7 %multiply_reduce_fusion.2 = (f32[16,4,128]{2,1,0:T(4,128)S(1)}, f32[16,4,128]{2,1,0:T(4,128)S(1)}) fusion(f32[16,32,4,128]{3,2,1,0:T(4,128)} %reshape.292, f32[16,32,4,128]{3,2,1,0:T(4,128)S(1)} %reshape.291, f32[16,32]{1,0:T(8,128)S(1)} %div.88, f32[16,32]{1,0:T(8,128)S(1)} %copy-done.13, f32[16,32]{1,0:T(8,128)S(1)} %copy-done.14), kind=kLoop, calls=%fused_computation.51 | loop fusion | flops 2605056 | bytes 2168832 | tf_op jit(solution)/shard_map/reduce_sum | solution.py:59
  225.4 97.1 %all-reduce.4.cloned.1.call-done = (f32[1024,128]{1,0:T(8,128)}, f32[1024,128]{1,0:T(8,128)}, f32[1024,128]{1,0:T(8,128)}, f32[1024,128]{1,0:T(8,128)}) async-done(((f32[1024,128]{1,0:T(8,128)}, f32[1024,128]{1,0:T(8,128)}, f32[1024,128]{1,0:T(8,128)}, f32[1024,128]{1,0:T(8,128)}), (f32[1024,128]{1,0:T(8,128)}, f32[1024,128]{1,0:T(8,128)}, f32[1024,128]{1,0:T(8,128)}, ...) | async-done | bytes 2097168 | tf_op jit(solution)/shard_map/psum | solution.py:143
  322.5 1.6 fusion.28
  324.1 1.7 convolution_bitcast_fusion
  (141 shorter events, 29.5 us)
Async XLA Ops:
  7.2 206.2 %copy-start = (bf16[512,1024]{1,0:T(8,128)(2,1)S(1)}, bf16[512,1024]{1,0:T(8,128)(2,1)}, u32[]{:S(2)}) copy-start(bf16[512,1024]{1,0:T(8,128)(2,1)} %param.23) | copy-start | bytes 3145732
  7.2 22.5 %copy-start.11 = (f32[1,1,1,16,128]{4,3,2,1,0:T(8,128)S(1)}, f32[1,1,1,16,128]{4,3,2,1,0:T(8,128)}, u32[]{:S(2)}) copy-start(f32[1,1,1,16,128]{4,3,2,1,0:T(8,128)} %param.27) | copy-start | bytes 24580
  7.2 315.3 %all-reduce.4.cloned.1.call-start = ((), (), s32[]{:S(2)}) async-start(), calls=%async_computation | async-start | bytes 4194304 | tf_op jit(solution)/shard_map/psum | solution.py:143
  9.5 122.7 %collective-permute-start.1 = (bf16[1,1,1,8,25,128]{5,4,3,2,1,0:T(8,128)(2,1)S(1)}, bf16[1,1,1,8,25,128]{5,4,3,2,1,0:T(8,128)(2,1)S(1)}, u32[]{:S(2)}, u32[]{:S(2)}) collective-permute-start(bf16[1,1,1,8,25,128]{5,4,3,2,1,0:T(8,128)(2,1)S(1)} %bitcast.173), channel_id=1, source_target_pairs={{64,0},{128,64},{192,128},{256,192},{320,256},{384,320},{448,384},... | collective-permute-start | bytes 153608 | tf_op jit(solution)/shard_map/ppermute | solution.py:23
  21.0 111.2 %collective-permute-start = (bf16[1,1,1,8,25,128]{5,4,3,2,1,0:T(8,128)(2,1)S(1)}, bf16[1,1,1,8,25,128]{5,4,3,2,1,0:T(8,128)(2,1)S(1)}, u32[]{:S(2)}, u32[]{:S(2)}) collective-permute-start(bf16[1,1,1,8,25,128]{5,4,3,2,1,0:T(8,128)(2,1)S(1)} %bitcast.174), channel_id=1, source_target_pairs={{0,64},{64,128},{128,192},{192,256},{256,320},{320,384},{384,448},... | collective-permute-start | bytes 153608 | tf_op jit(solution)/shard_map/ppermute | solution.py:20
  25.7 5.8 %copy-start.15 = (f32[1,1,1,3,512]{4,2,3,1,0:T(1,128)S(1)}, f32[1,1,1,3,512]{4,2,3,1,0:T(1,128)}, u32[]{:S(2)}) copy-start(f32[1,1,1,3,512]{4,2,3,1,0:T(1,128)} %param.21) | copy-start | bytes 18436
  25.7 5.9 %copy-start.20 = (s32[1,1,1,16,32]{4,3,2,1,0:T(8,128)S(1)}, s32[1,1,1,16,32]{4,3,2,1,0:T(8,128)}, u32[]{:S(2)}) copy-start(s32[1,1,1,16,32]{4,3,2,1,0:T(8,128)} %param.20) | copy-start | bytes 6148
  27.1 110.6 %copy-start.25 = (s32[5]{0:T(128)S(1)}, s32[5]{0:T(128)}, u32[]{:S(2)}) copy-start(s32[5]{0:T(128)} %constant.103) | copy-start | bytes 64
  27.1 110.6 %copy-start.23 = (s32[4]{0:T(128)S(1)}, s32[4]{0:T(128)}, u32[]{:S(2)}) copy-start(s32[4]{0:T(128)} %constant.105) | copy-start | bytes 52
  27.1 110.7 %copy-start.24 = (s32[4]{0:T(128)S(1)}, s32[4]{0:T(128)}, u32[]{:S(2)}) copy-start(s32[4]{0:T(128)} %constant.104) | copy-start | bytes 52
  31.5 119.8 %copy-start.21 = (s32[3]{0:T(128)S(1)}, s32[3]{0:T(128)}, u32[]{:S(2)}) copy-start(s32[3]{0:T(128)} %constant.107) | copy-start | bytes 40
  31.5 119.8 %copy-start.22 = (s32[3]{0:T(128)S(1)}, s32[3]{0:T(128)}, u32[]{:S(2)}) copy-start(s32[3]{0:T(128)} %constant.106) | copy-start | bytes 40
  31.5 120.0 %copy-start.8 = (bf16[640,640]{1,0:T(8,128)(2,1)S(1)}, bf16[640,640]{1,0:T(8,128)(2,1)}, u32[]{:S(2)}) copy-start(bf16[640,640]{1,0:T(8,128)(2,1)} %param.22) | copy-start | bytes 2457604
  132.2 7.0 %collective-permute-start.3 = (bf16[3,1,1,8,25,128]{5,4,3,2,1,0:T(8,128)(2,1)S(1)}, bf16[3,1,1,8,25,128]{5,4,3,2,1,0:T(8,128)(2,1)S(1)}, u32[]{:S(2)}, u32[]{:S(2)}) collective-permute-start(bf16[3,1,1,8,25,128]{5,4,3,2,1,0:T(8,128)(2,1)S(1)} %pad_maximum_fusion.3), channel_id=1, source_target_pairs={{8,0},{16,8},{24,16},{32,24},{40,32},{48,40},{56,48},{0,56},{9,1},... | collective-permute-start | bytes 460808 | tf_op jit(solution)/shard_map/ppermute | solution.py:23
  134.8 6.8 %collective-permute-start.2 = (bf16[3,1,1,8,25,128]{5,4,3,2,1,0:T(8,128)(2,1)S(1)}, bf16[3,1,1,8,25,128]{5,4,3,2,1,0:T(8,128)(2,1)S(1)}, u32[]{:S(2)}, u32[]{:S(2)}) collective-permute-start(bf16[3,1,1,8,25,128]{5,4,3,2,1,0:T(8,128)(2,1)S(1)} %pad_maximum_fusion.3), channel_id=1, source_target_pairs={{0,8},{8,16},{16,24},{24,32},{32,40},{40,48},{48,56},{56,0},{1,9},... | collective-permute-start | bytes 460808 | tf_op jit(solution)/shard_map/ppermute | solution.py:20
  141.9 17.3 %collective-permute-start.5 = (bf16[3,3,1,8,25,128]{5,3,4,2,1,0:T(8,128)(2,1)S(1)}, bf16[3,3,1,8,25,128]{5,3,4,2,1,0:T(8,128)(2,1)}, u32[]{:S(2)}, u32[]{:S(2)}) collective-permute-start(bf16[3,3,1,8,25,128]{5,3,4,2,1,0:T(8,128)(2,1)S(1)} %copy.50), channel_id=1, source_target_pairs={{1,0},{2,1},{3,2},{4,3},{5,4},{6,5},{7,6},{0,7},{9,8},{10,9},{11,1... | collective-permute-start | bytes 1382408 | tf_op jit(solution)/shard_map/ppermute | solution.py:23
  146.3 23.0 %collective-permute-start.4 = (bf16[3,3,1,8,25,128]{5,3,4,2,1,0:T(8,128)(2,1)S(1)}, bf16[3,3,1,8,25,128]{5,3,4,2,1,0:T(8,128)(2,1)}, u32[]{:S(2)}, u32[]{:S(2)}) collective-permute-start(bf16[3,3,1,8,25,128]{5,3,4,2,1,0:T(8,128)(2,1)S(1)} %copy.50), channel_id=1, source_target_pairs={{0,1},{1,2},{2,3},{3,4},{4,5},{5,6},{6,7},{7,0},{8,9},{9,10},{10,1... | collective-permute-start | bytes 1382408 | tf_op jit(solution)/shard_map/ppermute | solution.py:20
  198.5 2.2 copy-start.6
  202.1 2.5 copy-start.18
  202.1 2.5 copy-start.19
  209.8 3.2 copy-start.4
  209.8 3.2 copy-start.5
  209.8 3.2 copy-start.16
  209.9 3.2 copy-start.17
  216.5 4.2 %copy-start.13 = (f32[16,32]{1,0:T(8,128)S(1)}, f32[16,32]{1,0:T(8,128)}, u32[]{:S(2)}) copy-start(f32[16,32]{1,0:T(8,128)} %get-tuple-element.61) | copy-start | bytes 6148
  216.5 4.2 %copy-start.14 = (f32[16,32]{1,0:T(8,128)S(1)}, f32[16,32]{1,0:T(8,128)}, u32[]{:S(2)}) copy-start(f32[16,32]{1,0:T(8,128)} %get-tuple-element.62) | copy-start | bytes 6148
  218.1 6.6 %copy-start.10 = (bf16[1,1,1,16,25,128]{5,3,4,2,1,0:T(8,128)(2,1)S(1)}, bf16[1,1,1,16,25,128]{5,3,4,2,1,0:T(8,128)(2,1)}, u32[]{:S(2)}) copy-start(bf16[1,1,1,16,25,128]{5,3,4,2,1,0:T(8,128)(2,1)} %param.17) | copy-start | bytes 307204
  220.7 101.8 %copy-start.1 = (f32[1024,128]{1,0:T(8,128)S(1)}, f32[1024,128]{1,0:T(8,128)}, u32[]{:S(2)}) copy-start(f32[1024,128]{1,0:T(8,128)} %param.26) | copy-start | bytes 1572868
  322.5 3.3 copy-start.3
  325.8 1.4 copy-start.7
  326.7 2.4 copy-start.2
  327.2 2.4 copy-start.12
  (1 other events, 1.4 us)
Sparse Core Ops, SparseCore 0:
  31.6 290.8 all-reduce.3
where the time goes:
time: 340 us; the launch traced here: 339 us
  waiting for transfers between devices  115 us (34%)
  blocking collectives  100 us (29%)
  local copies, waits for them, and re-layouts  41.5 us (12%)
  starting transfers between devices  28.4 us (8%)
  matrix products  21.5 us (6%)
  other arithmetic  17.1 us (5%)
  between operations  14.8 us (4%)
    psum x1, blocking collectives, local(): lax.psum((table_product(cos_table, charges), table_product(sin_table, cha...  100 us
    psum x1, waiting for transfers between devices, local(): lax.psum((table_product(cos_table, charges), table_product(sin_table, cha...  97.1 us
    ppermute x3, starting transfers between devices, with_halo(): lax.ppermute(lax.slice_in_dim(block, 0, width, axis=dim), axis, backward)  18.5 us
    ppermute x3, waiting for transfers between devices, with_halo(): lax.ppermute(lax.slice_in_dim(block, block.shape[dim] - width, None, axis...  11.4 us
    ppermute x3, starting transfers between devices, with_halo(): lax.ppermute(lax.slice_in_dim(block, block.shape[dim] - width, None, axis...  9.83 us
    gather x2, local copies, waits for them, and re-layouts, edge_messages(): source = lookup_table[flat_index]  8.7 us
    dot_general x4, matrix products, table_product(): return jnp.dot(table.T, values, precision=highest)  7.13 us
  transfers between devices with their start and end apart: 7, of which 5 were waited for; matrix products, arithmetic and copies ran while one was open for 20% of the time, Pallas kernels for 0%

commit v1 on v0

v1 whole, which is shorter than its diff:
```python
import math

import jax
import jax.numpy as jnp
from jax import lax
from jax.experimental import pallas as pl
from jax.experimental.pallas import tpu as pltpu
from jax.sharding import PartitionSpec as P

MESH = pl.DeviceIdType.MESH
F32 = jnp.float32
BF16 = jnp.bfloat16

cell_length = 6.8
planar_floor = 0.25
radial_width = 64.0
atoms_total = 8192
wave_vectors = 1024
side = 8

GROUP = 16
PEERS = 32
CENTER = 13

half_zero = (0, 2, 6, 12, 20, 3, 7, 13, 21)
half_one = (1, 5, 11, 19, 8, 14, 22, 4, 10, 18)
untouched = (9, 15, 16, 17, 23, 24)


def split(values):
    high = values.astype(BF16)
    return high, (values - high.astype(F32)).astype(BF16)


def dot(a, b, dims=((1,), (0,))):
    return lax.dot_general(a, b, (dims, ((), ())), preferred_element_type=F32)


def dot3(a, b, dims=((1,), (0,))):
    a_high, a_low = split(a)
    b_high, b_low = split(b)
    return dot(a_high, b_high, dims) + (dot(a_high, b_low, dims) + dot(a_low, b_high, dims))


def cos_turns(turns):
    reduced = jnp.abs(turns - jnp.round(turns)) - 0.25
    square = reduced * reduced
    total = jnp.full_like(square, 0.0)
    for power in (13, 11, 9, 7, 5, 3, 1):
        sign = 1.0 if power % 4 == 1 else -1.0
        total = total * square + (-sign * (2.0 * math.pi) ** power / math.factorial(power))
    return total * reduced


def iota(shape, dim):
    return lax.broadcasted_iota(jnp.int32, shape, dim)


def kernel(
    node_ref,
    pos_ref,
    send_ref,
    nb_ref,
    disp_ref,
    w0_hbm,
    w1_hbm,
    w2_hbm,
    trip_ref,
    filt_hbm,
    cot_ref,
    out_ref,
    long_ref,
    charge_ref,
    pgrad_ref,
    table,
    w0,
    w1,
    w2,
    filt,
    atoms,
    trip,
    tiles,
    tiles_in,
    extra_in,
    summed,
    extra,
    part,
    part_in,
    load_sem,
    halo_send,
    halo_z,
    halo_y,
    halo_x,
    send_sem,
    recv_sem,
):
    px, py, pz = lax.axis_index("gx"), lax.axis_index("gy"), lax.axis_index("gz")
    group = (pz // 2) * 4 + (px % 2) * 2 + py % 2
    peer = (px // 2) * 8 + (py // 2) * 2 + pz % 2

    def place(g, r):
        return (
            (r // 8) * 2 + (g // 2) % 2,
            ((r // 2) % 4) * 2 + g % 2,
            (g // 4) * 2 + r % 2,
        )

    def mate(j):
        other = (group + j) % GROUP
        return other, place(other, peer)

    def fellow(j):
        other = (peer + j) % PEERS
        return other, place(group, other)

    around_x = ((px + 1) % side, py, pz), ((px + side - 1) % side, py, pz)
    around_y = (px, (py + 1) % side, pz), (px, (py + side - 1) % side, pz)
    around_z = (px, py, (pz + 1) % side), (px, py, (pz + side - 1) % side)

    def wait_bytes(ref, sem):
        pltpu.make_async_copy(ref, ref, sem).wait()

    barrier = pltpu.get_barrier_semaphore()

    def greet(device):
        pl.semaphore_signal(barrier, inc=1, device_id=device, device_id_type=MESH)

    def greet_mate(j, carry):
        greet(mate(j)[1])
        return carry

    def greet_fellow(j, carry):
        greet(fellow(j)[1])
        return carry

    lax.fori_loop(1, GROUP, greet_mate, 0)
    lax.fori_loop(1, PEERS, greet_fellow, 0)
    for device in around_x + around_y + around_z:
        greet(device)

    loads = [
        pltpu.make_async_copy(
            filt_hbm.at[pl.ds(pl.multiple_of(group * 64, 64), 64), :], filt, load_sem.at[0]
        ),
        pltpu.make_async_copy(w0_hbm, w0, load_sem.at[1]),
        pltpu.make_async_copy(w1_hbm, w1, load_sem.at[2]),
        pltpu.make_async_copy(w2_hbm, w2, load_sem.at[3]),
    ]
    for load in loads:
        load.start()

    atoms[group, 0:16, :] = node_ref[0].astype(F32)
    atoms[group, 16:32, :] = cot_ref[...]
    atoms[group, 32:40, :] = jnp.zeros((8, 128), F32)
    for axis, index in enumerate((px, py, pz)):
        corner = cell_length * index.astype(F32)
        atoms[group, 32 + axis : 33 + axis, 0:16] = (pos_ref[axis] + corner) / (
            cell_length * side
        )

    own_zero = jnp.concatenate(
        [node_ref[s] for s in half_zero] + [jnp.zeros((16, 128), BF16)], axis=1
    )
    own_one = jnp.concatenate([node_ref[s] for s in half_one], axis=1)
    sent = jnp.sum(
        jnp.where(
            iota((16, 8), 0) % 8 == iota((16, 8), 1),
            jnp.broadcast_to(send_ref[...], (16, 8)).astype(F32),
            0.0,
        ),
        axis=1,
        keepdims=True,
    )
    chosen = jnp.where(iota((16, 16), 1).astype(F32) == sent, 1.0, 0.0).astype(BF16)
    upper = iota((16, 1280), 0) < 8
    table[CENTER] = jnp.where(upper, dot(chosen, own_zero), dot(chosen, own_one)).astype(BF16)

    pl.semaphore_wait(barrier, GROUP - 1 + PEERS - 1 + 6)

    def send_atoms(j, carry):
        pltpu.make_async_remote_copy(
            src_ref=atoms.at[group],
            dst_ref=atoms.at[group],
            send_sem=send_sem.at[0],
            recv_sem=recv_sem.at[0],
            device_id=mate(j)[1],
            device_id_type=MESH,
        ).start()
        return carry

    lax.fori_loop(1, GROUP, send_atoms, 0)

    def pass_on(first, count, to, device, sem):
        pltpu.make_async_remote_copy(
            src_ref=table.at[pl.ds(first, count)],
            dst_ref=table.at[pl.ds(to, count)],
            send_sem=halo_send,
            recv_sem=sem,
            device_id=device,
            device_id_type=MESH,
        ).start()

    def along_z(first, count):
        pass_on(first, count, first - 1, around_z[0], halo_z.at[0])
        pass_on(first, count, first + 1, around_z[1], halo_z.at[1])

    def along_y(first, count):
        pass_on(first, count, first - 3, around_y[0], halo_y.at[0])
        pass_on(first, count, first + 3, around_y[1], halo_y.at[1])

    def along_x(first, count):
        pass_on(first, count, first - 9, around_x[0], halo_x.at[0])
        pass_on(first, count, first + 9, around_x[1], halo_x.at[1])

    along_z(CENTER, 1)
    along_y(CENTER, 1)
    along_x(CENTER, 1)

    own_zero_wide, own_one_wide = own_zero.astype(F32), own_one.astype(F32)
    for part_of in range(2):
        rows = slice(8 * part_of, 8 * part_of + 8)
        table[27 + part_of] = jnp.concatenate(
            [own_zero_wide[rows], own_one_wide[rows]], axis=0
        ).astype(BF16)
    for spare in range(29, 32):
        table[spare] = jnp.zeros((16, 1280), BF16)

    block = trip_ref[:, pl.ds(pl.multiple_of((group // 2) * 128, 128), 128)].astype(F32)
    trip[...] = jnp.zeros((8, 128), F32)
    trip[0:3, :] = block
    block = trip[...]
    triples = jnp.where(
        iota((8, 128), 1) // 64 == group % 2, block, pltpu.roll(block, 64, axis=1)
    )
    triples_down = triples.T

    d0, d1, d2 = disp_ref[0], disp_ref[1], disp_ref[2]
    radial = jnp.exp(-(d0 * d0 + d1 * d1 + d2 * d2) / radial_width) / math.sqrt(32)
    planar = jnp.sqrt(d0 * d0 + d1 * d1 + planar_floor)
    cos_one, sin_one = d0 / planar, d1 / planar
    cos_two, sin_two = cos_one * cos_one - sin_one * sin_one, 2.0 * cos_one * sin_one
    edge_weights = (
        radial,
        radial * (cos_one * cos_one + sin_one * sin_one),
        radial * (cos_two * cos_two + sin_two * sin_two),
    )
    of_atom = iota((16, 512), 1) // 32 == iota((16, 512), 0)
    repeat = jnp.where(iota((32, 512), 1) % 32 == iota((32, 512), 0), 1.0, 0.0).astype(BF16)
    named = dot(nb_ref[...].astype(F32).astype(BF16), repeat)
    named = jnp.sum(jnp.where(of_atom, named, 0.0), axis=0, keepdims=True)
    row = iota((512, 128), 0)
    place_of, atom_of = row // 16, row % 16
    listed = jnp.where(
        place_of < 27, 16 + 8 * place_of + atom_of, 8 * (place_of - 27) + atom_of
    )
    listed = jnp.where((atom_of < 8) & (place_of < 29), listed, -1).astype(F32)
    hits = jnp.concatenate(
        [
            jnp.where(named[:, 128 * b : 128 * b + 128] == listed, 1.0, 0.0).astype(BF16)
            for b in range(4)
        ],
        axis=1,
    )
    weight_rows = []
    for weight in edge_weights:
        for piece in split(jnp.where(of_atom, jnp.broadcast_to(weight, (16, 512)), 0.0)):
            weight_rows.append(piece)
    gathered = dot(jnp.concatenate(weight_rows, axis=0), hits, ((1,), (1,)))
    by_order = [gathered[32 * m : 32 * m + 16] + gathered[32 * m + 16 : 32 * m + 32] for m in range(3)]
    mixers = []
    for values in (
        by_order[0],
        by_order[1],
        pltpu.roll(by_order[1], 8, axis=1),
        pltpu.roll(by_order[2], 8, axis=1),
    ):
        mixers.extend(split(values))
    mixers = jnp.concatenate(mixers, axis=0)

    wait_bytes(atoms.at[pl.ds(0, GROUP - 1)], recv_sem.at[0])
    charges = atoms[:, 0:16, :].reshape(256, 128)
    grad_input = atoms[:, 16:32, :].reshape(256, 128)
    places = []
    for low in (0, 8):
        total = atoms[low, 32:40, :]
        for step in range(1, 8):
            total = total + pltpu.roll(atoms[low + step, 32:40, :], 16 * step, axis=1)
        places.append(total)
    places = jnp.concatenate(places, axis=1)
    turns = (
        triples_down[:, 0:1] * places[0:1, :]
        + triples_down[:, 1:2] * places[1:2, :]
        + triples_down[:, 2:3] * places[2:3, :]
    )
    is_sine = iota((128, 256), 0) >= 64
    waves = cos_turns(turns - jnp.where(is_sine, 0.25, 0.0))
    waves_high, waves_low = split(waves)
    charges_half = charges.astype(BF16)
    grad_high, grad_low = split(grad_input)
    raw = dot(waves_high, charges_half) + dot(waves_low, charges_half)
    response = dot(waves_high, grad_high) + (
        dot(waves_high, grad_low) + dot(waves_low, grad_high)
    )
    waves_across = waves.T
    tiles[0:16] = raw.reshape(16, 8, 128)
    tiles[16:32] = response.reshape(16, 8, 128)
    row8 = iota((8, 128), 0)
    tiles[32] = jnp.where(
        row8 == 0,
        jnp.sum(waves_across, axis=0, keepdims=True),
        jnp.where(row8 == 1, jnp.sum(charges, axis=0, keepdims=True), 0.0),
    )

    def send_tile(j, carry):
        other, device = fellow(j)
        pltpu.make_async_remote_copy(
            src_ref=tiles.at[other],
            dst_ref=tiles_in.at[j - 1],
            send_sem=send_sem.at[1],
            recv_sem=recv_sem.at[1],
            device_id=device,
            device_id_type=MESH,
        ).start()
        return carry

    @pl.when(peer != 0)
    def _():
        pltpu.make_async_remote_copy(
            src_ref=tiles.at[PEERS],
            dst_ref=extra_in.at[peer - 1],
            send_sem=send_sem.at[2],
            recv_sem=recv_sem.at[2],
            device_id=place(group, 0),
            device_id_type=MESH,
        ).start()

    lax.fori_loop(1, PEERS, send_tile, 0)

    wait_bytes(table.at[12], halo_z.at[0])
    wait_bytes(table.at[14], halo_z.at[1])
    for piece in (12, 14):
        along_y(piece, 1)
    for piece in (12, 14):
        along_x(piece, 1)

    wait_bytes(tiles_in, recv_sem.at[1])
    summed[peer] = tiles[peer] + jnp.sum(tiles_in[...], axis=0)

    def send_sum(j, carry):
        pltpu.make_async_remote_copy(
            src_ref=summed.at[peer],
            dst_ref=summed.at[peer],
            send_sem=send_sem.at[3],
            recv_sem=recv_sem.at[3],
            device_id=fellow(j)[1],
            device_id_type=MESH,
        ).start()
        return carry

    lax.fori_loop(1, PEERS, send_sum, 0)

    @pl.when(peer == 0)
    def _():
        wait_bytes(extra_in, recv_sem.at[2])
        extra[...] = tiles[PEERS] + jnp.sum(extra_in[...], axis=0)

        def send_extra(j, carry):
            pltpu.make_async_remote_copy(
                src_ref=extra,
                dst_ref=extra,
                send_sem=send_sem.at[4],
                recv_sem=recv_sem.at[4],
                device_id=fellow(j)[1],
                device_id_type=MESH,
            ).start()
            return carry

        lax.fori_loop(1, PEERS, send_extra, 0)

    wait_bytes(table.at[pl.ds(9, 3)], halo_y.at[0])
    along_x(9, 3)
    wait_bytes(table.at[pl.ds(15, 3)], halo_y.at[1])
    along_x(15, 3)

    scale = 1.0 / math.sqrt(atoms_total * wave_vectors)
    loads[0].wait()
    wait_bytes(summed.at[pl.ds(0, PEERS - 1)], recv_sem.at[3])

    @pl.when(peer != 0)
    def _():
        wait_bytes(extra, recv_sem.at[4])

    sums = extra[...]
    mean_charge = sums[1:2, :] / atoms_total
    plane_down = sums.T[:, 0:1]
    factor = filt[...] * scale
    factor = jnp.concatenate([factor, factor], axis=0)
    filtered = factor * (summed[0:16].reshape(128, 128) - plane_down * mean_charge)
    filtered_response = factor * summed[16:32].reshape(128, 128)
    long_part = dot3(waves_across, filtered)
    charge_part = dot3(waves_across - sums[0:1, :] / atoms_total, filtered_response)

    def swapped(values):
        return jnp.concatenate([values[64:], values[:64]], axis=0)

    both = jnp.concatenate([swapped(filtered), swapped(filtered_response)], axis=1)
    sides = jnp.concatenate([grad_input, charges - mean_charge], axis=1)
    phase_grad = waves * dot3(both, sides, ((1,), (1,)))
    signed = jnp.where(iota((8, 128), 1) < 64, triples, -triples).astype(BF16)
    phase_high, phase_low = split(phase_grad)
    pgrad = (dot(signed, phase_high) + dot(signed, phase_low)) * (
        2.0 * math.pi / (cell_length * side)
    )
    part[:, 0:16, :] = long_part.reshape(GROUP, 16, 128)
    part[:, 16:32, :] = charge_part.reshape(GROUP, 16, 128)
    for device in range(GROUP):
        low = 128 * (device // 8)
        values = pgrad[:, low : low + 128]
        if device % 8:
            values = pltpu.roll(values, 128 - 16 * (device % 8), axis=1)
        part[device, 32:40, :] = values

    def send_part(j, carry):
        other, device = mate(j)
        pltpu.make_async_remote_copy(
            src_ref=part.at[other],
            dst_ref=part_in.at[j - 1],
            send_sem=send_sem.at[5],
            recv_sem=recv_sem.at[5],
            device_id=device,
            device_id_type=MESH,
        ).start()
        return carry

    lax.fori_loop(1, GROUP, send_part, 0)

    wait_bytes(table.at[pl.ds(0, 9)], halo_x.at[0])
    wait_bytes(table.at[pl.ds(18, 9)], halo_x.at[1])
    collected = dot(mixers, table[...].reshape(512, 1280))

    def pair(first, lanes):
        return collected[first : first + 16, lanes] + collected[first + 16 : first + 32, lanes]

    loads[1].wait()
    mixed = dot(jnp.concatenate(split(pair(0, slice(0, 640))), axis=0), w0[...])
    mixed = mixed[0:16] + mixed[16:32]
    messages = {l * l + l: mixed[:, 128 * l : 128 * l + 128] for l in range(5)}
    for order, plus, minus, load, weights in (
        (1, pair(32, slice(640, 1152)), pair(64, slice(0, 512)), loads[2], w1),
        (2, pair(96, slice(512, 896)), pair(96, slice(896, 1280)), loads[3], w2),
    ):
        load.wait()
        wide = (5 - order) * 128
        product = dot(jnp.concatenate(split(plus) + split(minus), axis=0), weights[...])
        from_plus = product[0:16] + product[16:32]
        from_minus = product[32:48] + product[48:64]
        mixed_plus = from_plus[:, :wide] - from_minus[:, wide:]
        mixed_minus = from_minus[:, :wide] + from_plus[:, wide:]
        for at, degree in enumerate(range(order, 5)):
            center = degree * degree + degree
            messages[center + order] = mixed_plus[:, 128 * at : 128 * at + 128]
            messages[center - order] = mixed_minus[:, 128 * at : 128 * at + 128]
    for slot, message in messages.items():
        out_ref[slot] = (node_ref[slot].astype(F32) + message).astype(BF16)
    for slot in untouched:
        out_ref[slot] = node_ref[slot]

    wait_bytes(part_in, recv_sem.at[5])
    result = part[group] + jnp.sum(part_in[...], axis=0)
    long_ref[...] = result[0:16]
    charge_ref[...] = result[16:32]
    for axis in range(3):
        pgrad_ref[axis] = result[32 + axis : 33 + axis, 0:16]

    wait_bytes(table.at[pl.ds(0, 26)], halo_send)
    wait_bytes(part_in, send_sem.at[0])
    wait_bytes(tiles_in, send_sem.at[1])

    @pl.when(peer != 0)
    def _():
        wait_bytes(extra, send_sem.at[2])

    wait_bytes(tiles_in, send_sem.at[3])

    @pl.when(peer == 0)
    def _():
        wait_bytes(tiles_in, send_sem.at[4])

    wait_bytes(part_in, send_sem.at[5])


def local(
    node_irreps,
    positions,
    send_list,
    neighbours,
    displacements,
    order_zero,
    order_one,
    order_two,
    reciprocal_triples,
    reciprocal_filter,
    cotangent,
):
    vmem = pl.BlockSpec(memory_space=pltpu.VMEM)
    far = pl.BlockSpec(memory_space=pl.ANY)
    updated, long_range, charge_grad, position_grad = pl.pallas_call(
        kernel,
        out_shape=(
            jax.ShapeDtypeStruct((25, 16, 128), BF16),
            jax.ShapeDtypeStruct((16, 128), F32),
            jax.ShapeDtypeStruct((16, 128), F32),
            jax.ShapeDtypeStruct((3, 1, 16), F32),
        ),
        in_specs=[vmem, vmem, vmem, vmem, vmem, far, far, far, vmem, far, vmem],
        out_specs=(vmem, vmem, vmem, vmem),
        scratch_shapes=[
            pltpu.VMEM((32, 16, 1280), BF16),
            pltpu.VMEM((640, 640), BF16),
            pltpu.VMEM((512, 1024), BF16),
            pltpu.VMEM((384, 768), BF16),
            pltpu.VMEM((64, 128), F32),
            pltpu.VMEM((GROUP, 40, 128), F32),
            pltpu.VMEM((8, 128), F32),
            pltpu.VMEM((PEERS + 1, 8, 128), F32),
            pltpu.VMEM((PEERS - 1, 8, 128), F32),
            pltpu.VMEM((PEERS - 1, 8, 128), F32),
            pltpu.VMEM((PEERS, 8, 128), F32),
            pltpu.VMEM((8, 128), F32),
            pltpu.VMEM((GROUP, 40, 128), F32),
            pltpu.VMEM((GROUP - 1, 40, 128), F32),
            pltpu.SemaphoreType.DMA((4,)),
            pltpu.SemaphoreType.DMA,
            pltpu.SemaphoreType.DMA((2,)),
            pltpu.SemaphoreType.DMA((2,)),
            pltpu.SemaphoreType.DMA((2,)),
            pltpu.SemaphoreType.DMA((6,)),
            pltpu.SemaphoreType.DMA((6,)),
        ],
        compiler_params=pltpu.CompilerParams(
            collective_id=0, has_side_effects=True, vmem_limit_bytes=40 * 1024 * 1024
        ),
    )(
        jnp.transpose(node_irreps[0, 0, 0], (1, 0, 2)),
        positions.reshape(3, 1, 16),
        send_list.reshape(1, 8),
        neighbours.reshape(16, 32),
        displacements.reshape(3, 1, 512),
        order_zero,
        order_one,
        order_two,
        reciprocal_triples.T,
        reciprocal_filter,
        cotangent.reshape(16, 128),
    )
    return (
        jnp.transpose(updated, (1, 0, 2))[None, None, None],
        long_range[None, None, None],
        charge_grad[None, None, None],
        position_grad.reshape(1, 1, 1, 3, 16),
    )


def solution(mesh):
    by_block = ("gx", "gy", "gz")
    return jax.shard_map(
        local,
        mesh=mesh,
        in_specs=(
            P(*by_block, None, None, None),
            P(*by_block, None, None),
            P(*by_block, None),
            P(*by_block, None, None),
            P(*by_block, None, None),
            P(),
            P(),
            P(),
            P(),
            P(),
            P(*by_block, None, None),
        ),
        out_specs=(
            P(*by_block, None, None, None),
            P(*by_block, None, None),
            P(*by_block, None, None),
            P(*by_block, None, None),
        ),
        check_vma=False,
    )
```

time: 340 us -> 59 us (0.17)
  waiting for transfers between devices: 115 us -> 0 us
  blocking collectives: 100 us -> 0 us
  Pallas kernels: 0 us -> 47.3 us
  local copies, waits for them, and re-layouts: 41.5 us -> 10.6 us
  starting transfers between devices: 28.4 us -> 0 us
  matrix products: 21.5 us -> 0 us
  other arithmetic: 17.1 us -> 0 us
  between operations: 14.8 us -> 0.68 us
    psum x1 -> x0, blocking collectives: 100 us -> none  [local(): lax.psum((table_product(cos_table, charges), table_product(sin_table, cha...]
    psum x1 -> x0, waiting for transfers between devices: 97.1 us -> none  [local(): lax.psum((table_product(cos_table, charges), table_product(sin_table, cha...]
    pallas_call x0 -> x1, Pallas kernels: none -> 47.3 us  [local(): pl.pallas_call(kernel, out_shape=(jax.ShapeDtypeStruct((25, 16, 128), BF1...]
    ppermute x6 -> x0, starting transfers between devices: 28.4 us -> none  [the longest x3 18.5 us: with_halo(): lax.ppermute(lax.slice_in_dim(block, 0, width, axis=dim), axis, backward)]
    gather x9 -> x0, local copies, waits for them, and re-layouts: 25.5 us -> none  [the longest x2 8.7 us: edge_messages(): source = lookup_table[flat_index]]
    dot_general x19 -> x0, matrix products: 21.5 us -> none  [the longest x4 7.13 us: table_product(): return jnp.dot(table.T, values, precision=highest)]
    ppermute x6 -> x0, waiting for transfers between devices: 17.8 us -> none  [the longest x3 11.4 us: with_halo(): lax.ppermute(lax.slice_in_dim(block, block.shape[dim] - width, None, axis...]
    unnamed x77 -> x26, local copies, waits for them, and re-layouts: 3.07 us -> 10.6 us
  transfers between devices with their start and end apart: 7 -> 0, of which waited for: 5 -> 0; matrix products, arithmetic and copies ran while one was open for 20% -> 0% of each run, Pallas kernels for 0% -> 0%
where the time goes in v1:
time: 59 us; the launch traced here: 58.5 us
  Pallas kernels  47.3 us (80%)
  local copies, waits for them, and re-layouts  10.6 us (18%)
  between operations  0.68 us (1%)
    pallas_call x1, Pallas kernels, local(): pl.pallas_call(kernel, out_shape=(jax.ShapeDtypeStruct((25, 16, 128), BF1...  47.3 us
    unnamed x26, local copies, waits for them, and re-layouts  10.6 us

profile of v1, /device:TPU:1, one launch (start us, length us, event | category | flops | bytes accessed | tf_op | source)
XLA Modules:
  0.0 58.5 jit_solution(3224609032646906385)
XLA Ops:
  0.6 0.0 copy-start.6
  0.6 0.0 copy-start.9
  0.7 0.0 copy-start.10
  0.7 0.7 %copy-done.6 = s32[1,1,1,16,32]{4,3,2,1,0:T(8,128)S(1)} copy-done((s32[1,1,1,16,32]{4,3,2,1,0:T(8,128)S(1)}, s32[1,1,1,16,32]{4,3,2,1,0:T(8,128)}, u32[]{:S(2)}) %copy-start.6) | copy-done | bytes 2072
  1.3 0.0 copy-done.9
  1.3 0.0 copy-done.10
  1.3 0.0 copy-start
  1.3 1.2 %copy-done = bf16[512,1024]{1,0:T(8,128)(2,1)S(1)} copy-done((bf16[512,1024]{1,0:T(8,128)(2,1)S(1)}, bf16[512,1024]{1,0:T(8,128)(2,1)}, u32[]{:S(2)}) %copy-start) | copy-done | bytes 1048600
  2.6 0.0 copy-start.1
  2.6 1.1 %copy-done.1 = bf16[640,640]{1,0:T(8,128)(2,1)S(1)} copy-done((bf16[640,640]{1,0:T(8,128)(2,1)S(1)}, bf16[640,640]{1,0:T(8,128)(2,1)}, u32[]{:S(2)}) %copy-start.1) | copy-done | bytes 819224
  3.7 0.0 copy-start.2
  3.7 1.1 %copy-done.2 = bf16[384,768]{1,0:T(8,128)(2,1)S(1)} copy-done((bf16[384,768]{1,0:T(8,128)(2,1)S(1)}, bf16[384,768]{1,0:T(8,128)(2,1)}, u32[]{:S(2)}) %copy-start.2) | copy-done | bytes 589848
  4.8 0.0 copy-start.3
  4.8 1.0 %copy-done.3 = f32[1024,128]{1,0:T(8,128)S(1)} copy-done((f32[1024,128]{1,0:T(8,128)S(1)}, f32[1024,128]{1,0:T(8,128)}, u32[]{:S(2)}) %copy-start.3) | copy-done | bytes 524312
  5.8 0.0 copy-start.4
  5.8 0.9 %copy-done.4 = bf16[1,1,1,16,25,128]{5,3,4,2,1,0:T(8,128)(2,1)S(1)} copy-done((bf16[1,1,1,16,25,128]{5,3,4,2,1,0:T(8,128)(2,1)S(1)}, bf16[1,1,1,16,25,128]{5,3,4,2,1,0:T(8,128)(2,1)}, u32[]{:S(2)}) %copy-start.4) | copy-done | bytes 102424
  6.7 0.0 copy-start.5
  6.7 0.7 %copy-done.5 = s32[1024,3]{0,1:T(4,128)S(1)} copy-done((s32[1024,3]{0,1:T(4,128)S(1)}, s32[1024,3]{0,1:T(4,128)}, u32[]{:S(2)}) %copy-start.5) | copy-done | bytes 12312
  7.4 0.0 copy-start.7
  7.4 0.7 %copy-done.7 = f32[1,1,1,16,128]{4,3,2,1,0:T(8,128)S(1)} copy-done((f32[1,1,1,16,128]{4,3,2,1,0:T(8,128)S(1)}, f32[1,1,1,16,128]{4,3,2,1,0:T(8,128)}, u32[]{:S(2)}) %copy-start.7) | copy-done | bytes 8216
  8.1 0.0 copy-start.8
  8.1 0.7 %copy-done.8 = f32[1,1,1,3,512]{4,2,3,1,0:T(1,128)S(1)} copy-done((f32[1,1,1,3,512]{4,2,3,1,0:T(1,128)S(1)}, f32[1,1,1,3,512]{4,2,3,1,0:T(1,128)}, u32[]{:S(2)}) %copy-start.8) | copy-done | bytes 6168
  8.8 47.3 %shard_map.138 = (bf16[25,16,128]{2,1,0:T(8,128)(2,1)S(1)}, f32[16,128]{1,0:T(8,128)S(1)}, f32[16,128]{1,0:T(8,128)S(1)}, f32[3,1,16]{2,1,0:T(1,128)S(1)}) custom-call(bf16[25,16,128]{2,1,0:T(8,128)(2,1)S(1)} %bitcast.18, f32[3,1,16]{2,1,0:T(1,128)S(1)} %bitcast.25, s32[1,8]{1,0:T(1,128)S(1)} %bitcast.27, s32[16,32]{1,0:T(8,128)S(1)} %bitcast.20, ...), custom_call_target="tpu_custom_call" | custom-call | tf_op jit(solution)/shard_map/pallas_call | solution.py:507
  56.1 0.6 %copy.20 = bf16[1,1,1,16,25,128]{5,3,4,2,1,0:T(8,128)(2,1)} copy(bf16[1,1,1,16,25,128]{5,3,4,2,1,0:T(8,128)(2,1)S(1)} %bitcast.17) | data formatting | bytes 204800
  56.8 0.6 %copy.21 = f32[1,1,1,16,128]{4,3,2,1,0:T(8,128)} copy(f32[1,1,1,16,128]{4,3,2,1,0:T(8,128)S(1)} %bitcast.23) | data formatting | bytes 16384
  57.4 0.6 %copy.22 = f32[1,1,1,16,128]{4,3,2,1,0:T(8,128)} copy(f32[1,1,1,16,128]{4,3,2,1,0:T(8,128)S(1)} %bitcast.22) | data formatting | bytes 16384
  58.0 0.6 copy.23
Async XLA Ops:
  0.6 0.7 %copy-start.6 = (s32[1,1,1,16,32]{4,3,2,1,0:T(8,128)S(1)}, s32[1,1,1,16,32]{4,3,2,1,0:T(8,128)}, u32[]{:S(2)}) copy-start(s32[1,1,1,16,32]{4,3,2,1,0:T(8,128)} %param.14) | copy-start | bytes 6148
  0.6 0.7 %copy-start.9 = (f32[1,1,1,3,16]{4,2,3,1,0:T(1,128)S(1)}, f32[1,1,1,3,16]{4,2,3,1,0:T(1,128)}, u32[]{:S(2)}) copy-start(f32[1,1,1,3,16]{4,2,3,1,0:T(1,128)} %param.12) | copy-start | bytes 580
  0.7 0.7 %copy-start.10 = (s32[1,1,1,8]{3,2,1,0:T(1,128)S(1)}, s32[1,1,1,8]{3,2,1,0:T(1,128)}, u32[]{:S(2)}) copy-start(s32[1,1,1,8]{3,2,1,0:T(1,128)} %param.13) | copy-start | bytes 100
  1.3 1.2 %copy-start = (bf16[512,1024]{1,0:T(8,128)(2,1)S(1)}, bf16[512,1024]{1,0:T(8,128)(2,1)}, u32[]{:S(2)}) copy-start(bf16[512,1024]{1,0:T(8,128)(2,1)} %w1_hbm.1) | copy-start | bytes 3145732
  2.6 1.1 %copy-start.1 = (bf16[640,640]{1,0:T(8,128)(2,1)S(1)}, bf16[640,640]{1,0:T(8,128)(2,1)}, u32[]{:S(2)}) copy-start(bf16[640,640]{1,0:T(8,128)(2,1)} %w0_hbm.1) | copy-start | bytes 2457604
  3.7 1.1 %copy-start.2 = (bf16[384,768]{1,0:T(8,128)(2,1)S(1)}, bf16[384,768]{1,0:T(8,128)(2,1)}, u32[]{:S(2)}) copy-start(bf16[384,768]{1,0:T(8,128)(2,1)} %w2_hbm.1) | copy-start | bytes 1769476
  4.8 1.0 %copy-start.3 = (f32[1024,128]{1,0:T(8,128)S(1)}, f32[1024,128]{1,0:T(8,128)}, u32[]{:S(2)}) copy-start(f32[1024,128]{1,0:T(8,128)} %filt_hbm.1) | copy-start | bytes 1572868
  5.8 0.9 %copy-start.4 = (bf16[1,1,1,16,25,128]{5,3,4,2,1,0:T(8,128)(2,1)S(1)}, bf16[1,1,1,16,25,128]{5,3,4,2,1,0:T(8,128)(2,1)}, u32[]{:S(2)}) copy-start(bf16[1,1,1,16,25,128]{5,3,4,2,1,0:T(8,128)(2,1)} %param.11) | copy-start | bytes 307204
  6.7 0.7 %copy-start.5 = (s32[1024,3]{0,1:T(4,128)S(1)}, s32[1024,3]{0,1:T(4,128)}, u32[]{:S(2)}) copy-start(s32[1024,3]{0,1:T(4,128)} %param.19) | copy-start | bytes 36868
  7.4 0.7 %copy-start.7 = (f32[1,1,1,16,128]{4,3,2,1,0:T(8,128)S(1)}, f32[1,1,1,16,128]{4,3,2,1,0:T(8,128)}, u32[]{:S(2)}) copy-start(f32[1,1,1,16,128]{4,3,2,1,0:T(8,128)} %param.21) | copy-start | bytes 24580
  8.1 0.7 %copy-start.8 = (f32[1,1,1,3,512]{4,2,3,1,0:T(1,128)S(1)}, f32[1,1,1,3,512]{4,2,3,1,0:T(1,128)}, u32[]{:S(2)}) copy-start(f32[1,1,1,3,512]{4,2,3,1,0:T(1,128)} %param.15) | copy-start | bytes 18436

commit v2 on v1

v2 whole, which is shorter than its diff:
```python
import math

import jax
import jax.numpy as jnp
from jax import lax
from jax.experimental import pallas as pl
from jax.experimental.pallas import tpu as pltpu
from jax.sharding import PartitionSpec as P

MESH = pl.DeviceIdType.MESH
F32 = jnp.float32
BF16 = jnp.bfloat16

cell_length = 6.8
planar_floor = 0.25
radial_width = 64.0
atoms_total = 8192
wave_vectors = 1024
side = 8

GROUP = 16
PEERS = 32
CENTER = 13
ROWS = 10

half_zero = (0, 2, 6, 12, 20, 3, 7, 13, 21)
half_one = (1, 5, 11, 19, 8, 14, 22, 4, 10, 18)
untouched = (9, 15, 16, 17, 23, 24)


x_hops, y_hops = (0, 1, 2, 1), (0, 4, 1, 3, 2, 2, 2, 2)
mates = sorted(range(1, GROUP), key=lambda bits: -(x_hops[bits >> 2] + (bits >> 1) % 2))
fellows = sorted(
    range(1, PEERS), key=lambda bits: -(y_hops[bits % 8] + (0, 2, 4, 2)[bits >> 3])
)
along_ring = [bits for bits in fellows if bits < 8]
across_rings = [bits for bits in fellows if bits % 8 == 0]


def split(values):
    high = values.astype(BF16)
    return high, (values - high.astype(F32)).astype(BF16)


def dot(a, b, dims=((1,), (0,))):
    return lax.dot_general(a, b, (dims, ((), ())), preferred_element_type=F32)


def dot3(a, b, dims=((1,), (0,))):
    a_high, a_low = split(a)
    b_high, b_low = split(b)
    return dot(a_high, b_high, dims) + (dot(a_high, b_low, dims) + dot(a_low, b_high, dims))


def cos_turns(turns):
    reduced = jnp.abs(turns - jnp.round(turns)) - 0.25
    square = reduced * reduced
    total = jnp.full_like(square, 0.0)
    for power in (13, 11, 9, 7, 5, 3, 1):
        sign = 1.0 if power % 4 == 1 else -1.0
        total = total * square + (-sign * (2.0 * math.pi) ** power / math.factorial(power))
    return total * reduced


def iota(shape, dim):
    return lax.broadcasted_iota(jnp.int32, shape, dim)


def kernel(
    node_hbm,
    pos_hbm,
    send_hbm,
    nb_hbm,
    disp_hbm,
    w0_hbm,
    w1_hbm,
    w2_hbm,
    trip_hbm,
    filt_hbm,
    cot_hbm,
    out_hbm,
    long_hbm,
    charge_hbm,
    pgrad_hbm,
    first_ref,
    node_ref,
    pos_ref,
    send_ref,
    nb_ref,
    disp_ref,
    w0,
    w1,
    w2,
    trip_ref,
    filt,
    cot_ref,
    out_ref,
    result_ref,
    pgrad_ref,
    table,
    atoms,
    trip,
    tiles,
    tiles_in,
    summed,
    part,
    part_in,
    load_sem,
    store_sem,
    halo_send,
    halo_z,
    halo_y,
    halo_x,
    send_sem,
    recv_sem,
    ring_sem,
):
    px, py, pz = lax.axis_index("gx"), lax.axis_index("gy"), lax.axis_index("gz")
    group = (pz // 2) * 4 + (px % 2) * 2 + py % 2
    peer = (px // 2) * 8 + (py // 2) * 2 + pz % 2

    def turns_of(p):
        return 1 - 2 * (p % 2), 2 - 4 * ((p // 2) % 2), 4 - 8 * (p // 4)

    x_turns, y_turns, z_turns = turns_of(px), turns_of(py), turns_of(pz)
    group_turns = (y_turns[0], 2 * x_turns[0], 2 * z_turns[1], 2 * z_turns[2])
    peer_turns = (z_turns[0], y_turns[1], y_turns[2], 4 * x_turns[1], 4 * x_turns[2])

    def turned(start, bits, steps):
        for at, step in enumerate(steps):
            if (bits >> at) % 2:
                start = start + step
        return start

    def mate(bits):
        return turned(group, bits, group_turns), (
            turned(px, bits >> 1 & 1, x_turns),
            turned(py, bits & 1, y_turns),
            turned(pz, (bits >> 2) << 1, z_turns),
        )

    def fellow(bits):
        return turned(peer, bits, peer_turns), (
            turned(px, (bits >> 3) << 1, x_turns),
            turned(py, (bits >> 1 & 3) << 1, y_turns),
            turned(pz, bits & 1, z_turns),
        )

    around_x = ((px + 1) % side, py, pz), ((px + side - 1) % side, py, pz)
    around_y = (px, (py + 1) % side, pz), (px, (py + side - 1) % side, pz)
    around_z = (px, py, (pz + 1) % side), (px, py, (pz + side - 1) % side)

    def wait_bytes(ref, sem):
        pltpu.make_async_copy(ref, ref, sem).wait()

    slab = pl.multiple_of(group * 64, 64)
    loads = [
        pltpu.make_async_copy(source, target, load_sem.at[at])
        for at, (source, target) in enumerate(
            (
                (node_hbm.at[0], first_ref),
                (cot_hbm, cot_ref),
                (pos_hbm, pos_ref),
                (node_hbm, node_ref),
                (send_hbm, send_ref),
                (trip_hbm, trip_ref),
                (disp_hbm, disp_ref),
                (nb_hbm, nb_ref),
                (filt_hbm.at[pl.ds(slab, 64), :], filt),
                (w0_hbm, w0),
                (w1_hbm, w1),
                (w2_hbm, w2),
            )
        )
    ]
    for load in loads:
        load.start()

    barrier = pltpu.get_barrier_semaphore()

    def greet(device):
        pl.semaphore_signal(barrier, inc=1, device_id=device, device_id_type=MESH)

    for bits in along_ring + across_rings:
        greet(fellow(bits)[1])
    for device in around_z + around_y + around_x:
        greet(device)
    for bits in mates:
        greet(mate(bits)[1])

    for load in loads[:3]:
        load.wait()
    atoms[group, 0:16, :] = first_ref[...].astype(F32)
    atoms[group, 16:32, :] = cot_ref[...]
    atoms[group, 32:40, :] = jnp.zeros((8, 128), F32)
    for axis, index in enumerate((px, py, pz)):
        corner = cell_length * index.astype(F32)
        atoms[group, 32 + axis : 33 + axis, 0:16] = (pos_ref[axis] + corner) / (
            cell_length * side
        )

    pl.semaphore_wait(barrier, len(mates) + len(along_ring) + len(across_rings) + 6)

    for bits in mates:
        pltpu.make_async_remote_copy(
            src_ref=atoms.at[group],
            dst_ref=atoms.at[group],
            send_sem=send_sem.at[0],
            recv_sem=recv_sem.at[0],
            device_id=mate(bits)[1],
            device_id_type=MESH,
        ).start()

    for bits in across_rings:
        pl.semaphore_signal(
            ring_sem, inc=1, device_id=fellow(bits)[1], device_id_type=MESH
        )

    for load in loads[3:5]:
        load.wait()
    own_zero = jnp.concatenate(
        [node_ref[s] for s in half_zero] + [jnp.zeros((16, 128), BF16)], axis=1
    )
    own_one = jnp.concatenate([node_ref[s] for s in half_one], axis=1)
    sent = jnp.sum(
        jnp.where(
            iota((16, 8), 0) % 8 == iota((16, 8), 1),
            jnp.broadcast_to(send_ref[...], (16, 8)).astype(F32),
            0.0,
        ),
        axis=1,
        keepdims=True,
    )
    chosen = jnp.where(iota((16, 16), 1).astype(F32) == sent, 1.0, 0.0).astype(BF16)
    upper = iota((16, 1280), 0) < 8
    table[CENTER] = jnp.where(upper, dot(chosen, own_zero), dot(chosen, own_one)).astype(BF16)

    def pass_on(first, count, to, device, sem):
        pltpu.make_async_remote_copy(
            src_ref=table.at[pl.ds(first, count)],
            dst_ref=table.at[pl.ds(to, count)],
            send_sem=halo_send,
            recv_sem=sem,
            device_id=device,
            device_id_type=MESH,
        ).start()

    def along_z(first, count):
        pass_on(first, count, first - 1, around_z[0], halo_z.at[0])
        pass_on(first, count, first + 1, around_z[1], halo_z.at[1])

    def along_y(first, count):
        pass_on(first, count, first - 3, around_y[0], halo_y.at[0])
        pass_on(first, count, first + 3, around_y[1], halo_y.at[1])

    def along_x(first, count):
        pass_on(first, count, first - 9, around_x[0], halo_x.at[0])
        pass_on(first, count, first + 9, around_x[1], halo_x.at[1])

    along_z(CENTER, 1)
    along_y(CENTER, 1)
    along_x(CENTER, 1)

    own_zero_wide, own_one_wide = own_zero.astype(F32), own_one.astype(F32)
    for part_of in range(2):
        rows = slice(8 * part_of, 8 * part_of + 8)
        table[27 + part_of] = jnp.concatenate(
            [own_zero_wide[rows], own_one_wide[rows]], axis=0
        ).astype(BF16)
    for spare in range(29, 32):
        table[spare] = jnp.zeros((16, 1280), BF16)

    for load in loads[5:8]:
        load.wait()
    block = trip_ref[:, pl.ds(pl.multiple_of((group // 2) * 128, 128), 128)].astype(F32)
    trip[...] = jnp.zeros((8, 128), F32)
    trip[0:3, :] = block
    block = trip[...]
    triples = jnp.where(
        iota((8, 128), 1) // 64 == group % 2, block, pltpu.roll(block, 64, axis=1)
    )
    triples_down = triples.T

    d0, d1, d2 = disp_ref[0], disp_ref[1], disp_ref[2]
    radial = jnp.exp(-(d0 * d0 + d1 * d1 + d2 * d2) / radial_width) / math.sqrt(32)
    planar = jnp.sqrt(d0 * d0 + d1 * d1 + planar_floor)
    cos_one, sin_one = d0 / planar, d1 / planar
    cos_two, sin_two = cos_one * cos_one - sin_one * sin_one, 2.0 * cos_one * sin_one
    edge_weights = (
        radial,
        radial * (cos_one * cos_one + sin_one * sin_one),
        radial * (cos_two * cos_two + sin_two * sin_two),
    )
    of_atom = iota((16, 512), 1) // 32 == iota((16, 512), 0)
    repeat = jnp.where(iota((32, 512), 1) % 32 == iota((32, 512), 0), 1.0, 0.0).astype(BF16)
    named = dot(nb_ref[...].astype(F32).astype(BF16), repeat)
    named = jnp.sum(jnp.where(of_atom, named, 0.0), axis=0, keepdims=True)
    row = iota((512, 128), 0)
    place_of, atom_of = row // 16, row % 16
    listed = jnp.where(
        place_of < 27, 16 + 8 * place_of + atom_of, 8 * (place_of - 27) + atom_of
    )
    listed = jnp.where((atom_of < 8) & (place_of < 29), listed, -1).astype(F32)
    hits = jnp.concatenate(
        [
            jnp.where(named[:, 128 * b : 128 * b + 128] == listed, 1.0, 0.0).astype(BF16)
            for b in range(4)
        ],
        axis=1,
    )
    weight_rows = []
    for weight in edge_weights:
        for piece in split(jnp.where(of_atom, jnp.broadcast_to(weight, (16, 512)), 0.0)):
            weight_rows.append(piece)
    gathered = dot(jnp.concatenate(weight_rows, axis=0), hits, ((1,), (1,)))
    by_order = [gathered[32 * m : 32 * m + 16] + gathered[32 * m + 16 : 32 * m + 32] for m in range(3)]
    mixers = []
    for values in (
        by_order[0],
        by_order[1],
        pltpu.roll(by_order[1], 8, axis=1),
        pltpu.roll(by_order[2], 8, axis=1),
    ):
        mixers.extend(split(values))
    mixers = jnp.concatenate(mixers, axis=0)

    wait_bytes(atoms.at[pl.ds(0, GROUP - 1)], recv_sem.at[0])
    charges = atoms[:, 0:16, :].reshape(256, 128)
    grad_input = atoms[:, 16:32, :].reshape(256, 128)
    places = []
    for low in (0, 8):
        total = atoms[low, 32:40, :]
        for step in range(1, 8):
            total = total + pltpu.roll(atoms[low + step, 32:40, :], 16 * step, axis=1)
        places.append(total)
    places = jnp.concatenate(places, axis=1)
    turns = (
        triples_down[:, 0:1] * places[0:1, :]
        + triples_down[:, 1:2] * places[1:2, :]
        + triples_down[:, 2:3] * places[2:3, :]
    )
    is_sine = iota((128, 256), 0) >= 64
    waves = cos_turns(turns - jnp.where(is_sine, 0.25, 0.0))
    waves_high, waves_low = split(waves)
    charges_half = charges.astype(BF16)
    grad_high, grad_low = split(grad_input)
    raw = dot(waves_high, charges_half) + dot(waves_low, charges_half)
    response = dot(waves_high, grad_high) + (
        dot(waves_high, grad_low) + dot(waves_low, grad_high)
    )
    waves_across = waves.T
    tiles[0:16, 0:8, :] = raw.reshape(16, 8, 128)
    tiles[16:32, 0:8, :] = response.reshape(16, 8, 128)
    plane = jnp.sum(waves_across, axis=0, keepdims=True)
    total_charge = jnp.sum(charges, axis=0, keepdims=True)
    extra = jnp.concatenate([plane, total_charge, jnp.zeros((6, 128), F32)], axis=0)
    tiles[:, 8:16, :] = jnp.broadcast_to(extra, (PEERS, 8, 128))

    pl.semaphore_wait(ring_sem, len(across_rings))

    for bits in fellows:
        other, device = fellow(bits)
        pltpu.make_async_remote_copy(
            src_ref=tiles.at[other, pl.ds(0, ROWS)],
            dst_ref=tiles_in.at[bits - 1, pl.ds(0, ROWS)],
            send_sem=send_sem.at[1],
            recv_sem=recv_sem.at[1],
            device_id=device,
            device_id_type=MESH,
        ).start()

    wait_bytes(table.at[12], halo_z.at[0])
    wait_bytes(table.at[14], halo_z.at[1])
    for piece in (12, 14):
        along_y(piece, 1)
    for piece in (12, 14):
        along_x(piece, 1)

    wait_bytes(table.at[pl.ds(9, 3)], halo_y.at[0])
    along_x(9, 3)
    wait_bytes(table.at[pl.ds(15, 3)], halo_y.at[1])
    along_x(15, 3)

    all_tiles = tiles_in.at[:, pl.ds(0, ROWS), :]
    wait_bytes(all_tiles, recv_sem.at[1])
    whole = tiles[peer, 0:ROWS, :] + jnp.sum(tiles_in[:, 0:ROWS, :], axis=0)
    summed[peer] = whole[0:8]
    plane, total_charge = whole[8:9], whole[9:10]
    for bits in fellows:
        pltpu.make_async_remote_copy(
            src_ref=summed.at[peer],
            dst_ref=summed.at[peer],
            send_sem=send_sem.at[2],
            recv_sem=recv_sem.at[2],
            device_id=fellow(bits)[1],
            device_id_type=MESH,
        ).start()

    wait_bytes(table.at[pl.ds(0, 9)], halo_x.at[0])
    wait_bytes(table.at[pl.ds(18, 9)], halo_x.at[1])
    collected = dot(mixers, table[...].reshape(512, 1280))

    def pair(first, lanes):
        return collected[first : first + 16, lanes] + collected[first + 16 : first + 32, lanes]

    loads[9].wait()
    mixed = dot(jnp.concatenate(split(pair(0, slice(0, 640))), axis=0), w0[...])
    mixed = mixed[0:16] + mixed[16:32]
    messages = {l * l + l: mixed[:, 128 * l : 128 * l + 128] for l in range(5)}
    for order, plus, minus, load, weights in (
        (1, pair(32, slice(640, 1152)), pair(64, slice(0, 512)), loads[10], w1),
        (2, pair(96, slice(512, 896)), pair(96, slice(896, 1280)), loads[11], w2),
    ):
        load.wait()
        wide = (5 - order) * 128
        product = dot(jnp.concatenate(split(plus) + split(minus), axis=0), weights[...])
        from_plus = product[0:16] + product[16:32]
        from_minus = product[32:48] + product[48:64]
        mixed_plus = from_plus[:, :wide] - from_minus[:, wide:]
        mixed_minus = from_minus[:, :wide] + from_plus[:, wide:]
        for at, degree in enumerate(range(order, 5)):
            center = degree * degree + degree
            messages[center + order] = mixed_plus[:, 128 * at : 128 * at + 128]
            messages[center - order] = mixed_minus[:, 128 * at : 128 * at + 128]
    for slot, message in messages.items():
        out_ref[slot] = (node_ref[slot].astype(F32) + message).astype(BF16)
    for slot in untouched:
        out_ref[slot] = node_ref[slot]

    scale = 1.0 / math.sqrt(atoms_total * wave_vectors)
    loads[8].wait()
    wait_bytes(summed.at[pl.ds(0, PEERS - 1)], recv_sem.at[2])
    mean_charge = total_charge / atoms_total
    plane_down = jnp.broadcast_to(plane, (8, 128)).T[:, 0:1]
    factor = filt[...] * scale
    factor = jnp.concatenate([factor, factor], axis=0)
    filtered = factor * (summed[0:16].reshape(128, 128) - plane_down * mean_charge)
    filtered_response = factor * summed[16:32].reshape(128, 128)
    long_part = dot3(waves_across, filtered)
    charge_part = dot3(waves_across - plane / atoms_total, filtered_response)

    def swapped(values):
        return jnp.concatenate([values[64:], values[:64]], axis=0)

    both = jnp.concatenate([swapped(filtered), swapped(filtered_response)], axis=1)
    sides = jnp.concatenate([grad_input, charges - mean_charge], axis=1)
    phase_grad = waves * dot3(both, sides, ((1,), (1,)))
    signed = jnp.where(iota((8, 128), 1) < 64, triples, -triples).astype(BF16)
    phase_high, phase_low = split(phase_grad)
    pgrad = (dot(signed, phase_high) + dot(signed, phase_low)) * (
        2.0 * math.pi / (cell_length * side)
    )
    part[:, 0:16, :] = long_part.reshape(GROUP, 16, 128)
    part[:, 16:32, :] = charge_part.reshape(GROUP, 16, 128)
    for device in range(GROUP):
        low = 128 * (device // 8)
        values = pgrad[:, low : low + 128]
        if device % 8:
            values = pltpu.roll(values, 128 - 16 * (device % 8), axis=1)
        part[device, 32:40, :] = values

    for bits in mates:
        other, device = mate(bits)
        pltpu.make_async_remote_copy(
            src_ref=part.at[other],
            dst_ref=part_in.at[bits - 1],
            send_sem=send_sem.at[3],
            recv_sem=recv_sem.at[3],
            device_id=device,
            device_id_type=MESH,
        ).start()

    stores = [
        pltpu.make_async_copy(source, target, store_sem.at[at])
        for at, (source, target) in enumerate(
            (
                (out_ref, out_hbm),
                (result_ref.at[pl.ds(0, 16)], long_hbm),
                (result_ref.at[pl.ds(16, 16)], charge_hbm),
                (pgrad_ref, pgrad_hbm),
            )
        )
    ]
    stores[0].start()

    wait_bytes(part_in, recv_sem.at[3])
    result = part[group] + jnp.sum(part_in[...], axis=0)
    result_ref[...] = result
    for axis in range(3):
        pgrad_ref[axis] = result[32 + axis : 33 + axis, 0:16]
    for store in stores[1:]:
        store.start()

    wait_bytes(table.at[pl.ds(0, 26)], halo_send)
    wait_bytes(part_in, send_sem.at[0])
    wait_bytes(all_tiles, send_sem.at[1])
    wait_bytes(summed.at[pl.ds(0, PEERS - 1)], send_sem.at[2])
    wait_bytes(part_in, send_sem.at[3])
    for store in stores:
        store.wait()


def settle(*refs):
    sources, targets, held, sems = refs[0:4], refs[4:8], refs[8:12], refs[12]
    into = [pltpu.make_async_copy(sources[at], held[at], sems.at[at]) for at in range(4)]
    out = [pltpu.make_async_copy(held[at], targets[at], sems.at[4 + at]) for at in range(4)]
    for copy in into:
        copy.start()
    for arrive, leave in zip(into, out):
        arrive.wait()
        leave.start()
    for copy in out:
        copy.wait()


def local(
    node_irreps,
    positions,
    send_list,
    neighbours,
    displacements,
    order_zero,
    order_one,
    order_two,
    reciprocal_triples,
    reciprocal_filter,
    cotangent,
):
    far = pl.BlockSpec(memory_space=pl.ANY)
    results = (
        jax.ShapeDtypeStruct((25, 16, 128), BF16),
        jax.ShapeDtypeStruct((16, 128), F32),
        jax.ShapeDtypeStruct((16, 128), F32),
        jax.ShapeDtypeStruct((3, 1, 16), F32),
    )
    held = pl.pallas_call(
        kernel,
        out_shape=results,
        in_specs=[far] * 11,
        out_specs=(far,) * 4,
        scratch_shapes=[
            pltpu.VMEM((16, 128), BF16),
            pltpu.VMEM((25, 16, 128), BF16),
            pltpu.VMEM((3, 1, 16), F32),
            pltpu.VMEM((1, 8), jnp.int32),
            pltpu.VMEM((16, 32), jnp.int32),
            pltpu.VMEM((3, 1, 512), F32),
            pltpu.VMEM((640, 640), BF16),
            pltpu.VMEM((512, 1024), BF16),
            pltpu.VMEM((384, 768), BF16),
            pltpu.VMEM((3, 1024), jnp.int32),
            pltpu.VMEM((64, 128), F32),
            pltpu.VMEM((16, 128), F32),
            pltpu.VMEM((25, 16, 128), BF16),
            pltpu.VMEM((40, 128), F32),
            pltpu.VMEM((3, 1, 16), F32),
            pltpu.VMEM((32, 16, 1280), BF16),
            pltpu.VMEM((GROUP, 40, 128), F32),
            pltpu.VMEM((8, 128), F32),
            pltpu.VMEM((PEERS, 16, 128), F32),
            pltpu.VMEM((PEERS - 1, 16, 128), F32),
            pltpu.VMEM((PEERS, 8, 128), F32),
            pltpu.VMEM((GROUP, 40, 128), F32),
            pltpu.VMEM((GROUP - 1, 40, 128), F32),
            pltpu.SemaphoreType.DMA((12,)),
            pltpu.SemaphoreType.DMA((4,)),
            pltpu.SemaphoreType.DMA,
            pltpu.SemaphoreType.DMA((2,)),
            pltpu.SemaphoreType.DMA((2,)),
            pltpu.SemaphoreType.DMA((2,)),
            pltpu.SemaphoreType.DMA((4,)),
            pltpu.SemaphoreType.DMA((4,)),
            pltpu.SemaphoreType.REGULAR,
        ],
        compiler_params=pltpu.CompilerParams(
            collective_id=0, has_side_effects=True, vmem_limit_bytes=60 * 1024 * 1024
        ),
    )(
        jnp.transpose(node_irreps[0, 0, 0], (1, 0, 2)),
        positions.reshape(3, 1, 16),
        send_list.reshape(1, 8),
        neighbours.reshape(16, 32),
        displacements.reshape(3, 1, 512),
        order_zero,
        order_one,
        order_two,
        reciprocal_triples.T,
        reciprocal_filter,
        cotangent.reshape(16, 128),
    )
    updated, long_range, charge_grad, position_grad = pl.pallas_call(
        settle,
        out_shape=results,
        in_specs=[far] * 4,
        out_specs=(far,) * 4,
        scratch_shapes=[pltpu.VMEM(held_one.shape, held_one.dtype) for held_one in results]
        + [pltpu.SemaphoreType.DMA((8,))],
        compiler_params=pltpu.CompilerParams(vmem_limit_bytes=60 * 1024 * 1024),
    )(*held)
    return (
        jnp.transpose(updated, (1, 0, 2))[None, None, None],
        long_range[None, None, None],
        charge_grad[None, None, None],
        position_grad.reshape(1, 1, 1, 3, 16),
    )


def solution(mesh):
    by_block = ("gx", "gy", "gz")
    return jax.shard_map(
        local,
        mesh=mesh,
        in_specs=(
            P(*by_block, None, None, None),
            P(*by_block, None, None),
            P(*by_block, None),
            P(*by_block, None, None),
            P(*by_block, None, None),
            P(),
            P(),
            P(),
            P(),
            P(),
            P(*by_block, None, None),
        ),
        out_specs=(
            P(*by_block, None, None, None),
            P(*by_block, None, None),
            P(*by_block, None, None),
            P(*by_block, None, None),
        ),
        check_vma=False,
    )
```

time: 59 us -> 49.1 us (0.83)
  local copies, waits for them, and re-layouts: 10.6 us -> 0 us
  Pallas kernels: 47.3 us -> 48.3 us
    unnamed x26 -> x0, local copies, waits for them, and re-layouts: 10.6 us -> none
    pallas_call x1 -> x2, Pallas kernels: 47.3 us -> 48.3 us  [the longest x1 46.7 us: local(): pl.pallas_call(kernel, out_shape=results, in_specs=[far] * 11, out_specs=...]
where the time goes in v2:
time: 49.1 us; the launch traced here: 48.9 us
  Pallas kernels  48.3 us (98%)
  between operations  0.64 us (1%)
    pallas_call x1, Pallas kernels, local(): pl.pallas_call(kernel, out_shape=results, in_specs=[far] * 11, out_specs=...  46.7 us
    pallas_call x1, Pallas kernels, local(): pl.pallas_call(settle, out_shape=results, in_specs=[far] * 4, out_specs=(...  1.61 us

profile of v2, /device:TPU:1, one launch (start us, length us, event | category | flops | bytes accessed | tf_op | source)
XLA Modules:
  0.0 48.9 jit_solution(5756343265924390927)
XLA Ops:
  0.6 46.7 %shard_map.138 = (bf16[25,16,128]{2,1,0:T(8,128)(2,1)}, f32[16,128]{1,0:T(8,128)}, f32[16,128]{1,0:T(8,128)}, f32[3,1,16]{2,1,0:T(1,128)}) custom-call(bf16[25,16,128]{2,1,0:T(8,128)(2,1)} %bitcast.17, f32[3,1,16]{2,1,0:T(1,128)} %bitcast.22, s32[1,8]{1,0:T(1,128)} %bitcast.23, s32[16,32]{1,0:T(8,128)} %bitcast.19, f32[3,1,512]{2,1,0:T(1,128)} %bitcast.21, ...), custom_call_target="tpu_custom_call" | custom-call | tf_op jit(solution)/shard_map/pallas_call | solution.py:536
  47.3 1.6 %shard_map.139 = (bf16[25,16,128]{2,1,0:T(8,128)(2,1)}, f32[16,128]{1,0:T(8,128)}, f32[16,128]{1,0:T(8,128)}, f32[3,1,16]{2,1,0:T(1,128)}) custom-call(bf16[25,16,128]{2,1,0:T(8,128)(2,1)} %get-tuple-element.12.refs_0_, f32[16,128]{1,0:T(8,128)} %get-tuple-element.13.refs_1_, f32[16,128]{1,0:T(8,128)} %get-tuple-element.14.refs_2_, ...), custom_call_target="tpu_custom_call" | custom-call | tf_op jit(solution)/shard_map/pallas_call | solution.py:591

commit v3 on v2

--- a/solution.py
+++ b/solution.py
@@ -376,11 +376,6 @@
     for piece in (12, 14):
         along_x(piece, 1)
 
-    wait_bytes(table.at[pl.ds(9, 3)], halo_y.at[0])
-    along_x(9, 3)
-    wait_bytes(table.at[pl.ds(15, 3)], halo_y.at[1])
-    along_x(15, 3)
-
     all_tiles = tiles_in.at[:, pl.ds(0, ROWS), :]
     wait_bytes(all_tiles, recv_sem.at[1])
     whole = tiles[peer, 0:ROWS, :] + jnp.sum(tiles_in[:, 0:ROWS, :], axis=0)
@@ -393,6 +388,54 @@
             send_sem=send_sem.at[2],
             recv_sem=recv_sem.at[2],
             device_id=fellow(bits)[1],
+            device_id_type=MESH,
+        ).start()
+
+    wait_bytes(table.at[pl.ds(9, 3)], halo_y.at[0])
+    along_x(9, 3)
+    wait_bytes(table.at[pl.ds(15, 3)], halo_y.at[1])
+    along_x(15, 3)
+
+    scale = 1.0 / math.sqrt(atoms_total * wave_vectors)
+    loads[8].wait()
+    wait_bytes(summed.at[pl.ds(0, PEERS - 1)], recv_sem.at[2])
+    mean_charge = total_charge / atoms_total
+    plane_down = jnp.broadcast_to(plane, (8, 128)).T[:, 0:1]
+    factor = filt[...] * scale
+    factor = jnp.concatenate([factor, factor], axis=0)
+    filtered = factor * (summed[0:16].reshape(128, 128) - plane_down * mean_charge)
+    filtered_response = factor * summed[16:32].reshape(128, 128)
+    long_part = dot3(waves_across, filtered)
+    charge_part = dot3(waves_across - plane / atoms_total, filtered_response)
+
+    def swapped(values):
+        return jnp.concatenate([values[64:], values[:64]], axis=0)
+
+    both = jnp.concatenate([swapped(filtered), swapped(filtered_response)], axis=1)
+    sides = jnp.concatenate([grad_input, charges - mean_charge], axis=1)
+    phase_grad = waves * dot3(both, sides, ((1,), (1,)))
+    signed = jnp.where(iota((8, 128), 1) < 64, triples, -triples).astype(BF16)
+    phase_high, phase_low = split(phase_grad)
+    pgrad = (dot(signed, phase_high) + dot(signed, phase_low)) * (
+        2.0 * math.pi / (cell_length * side)
+    )
+    part[:, 0:16, :] = long_part.reshape(GROUP, 16, 128)
+    part[:, 16:32, :] = charge_part.reshape(GROUP, 16, 128)
+    for device in range(GROUP):
+        low = 128 * (device // 8)
+        values = pgrad[:, low : low + 128]
+        if device % 8:
+            values = pltpu.roll(values, 128 - 16 * (device % 8), axis=1)
+        part[device, 32:40, :] = values
+
+    for bits in mates:
+        other, device = mate(bits)
+        pltpu.make_async_remote_copy(
+            src_ref=part.at[other],
+            dst_ref=part_in.at[bits - 1],
+            send_sem=send_sem.at[3],
+            recv_sem=recv_sem.at[3],
+            device_id=device,
             device_id_type=MESH,
         ).start()
 
@@ -426,49 +469,6 @@
         out_ref[slot] = (node_ref[slot].astype(F32) + message).astype(BF16)
     for slot in untouched:
         out_ref[slot] = node_ref[slot]
-
-    scale = 1.0 / math.sqrt(atoms_total * wave_vectors)
-    loads[8].wait()
-    wait_bytes(summed.at[pl.ds(0, PEERS - 1)], recv_sem.at[2])
-    mean_charge = total_charge / atoms_total
-    plane_down = jnp.broadcast_to(plane, (8, 128)).T[:, 0:1]
-    factor = filt[...] * scale
-    factor = jnp.concatenate([factor, factor], axis=0)
-    filtered = factor * (summed[0:16].reshape(128, 128) - plane_down * mean_charge)
-    filtered_response = factor * summed[16:32].reshape(128, 128)
-    long_part = dot3(waves_across, filtered)
-    charge_part = dot3(waves_across - plane / atoms_total, filtered_response)
-
-    def swapped(values):
-        return jnp.concatenate([values[64:], values[:64]], axis=0)
-
-    both = jnp.concatenate([swapped(filtered), swapped(filtered_response)], axis=1)
-    sides = jnp.concatenate([grad_input, charges - mean_charge], axis=1)
-    phase_grad = waves * dot3(both, sides, ((1,), (1,)))
-    signed = jnp.where(iota((8, 128), 1) < 64, triples, -triples).astype(BF16)
-    phase_high, phase_low = split(phase_grad)
-    pgrad = (dot(signed, phase_high) + dot(signed, phase_low)) * (
-        2.0 * math.pi / (cell_length * side)
-    )
-    part[:, 0:16, :] = long_part.reshape(GROUP, 16, 128)
-    part[:, 16:32, :] = charge_part.reshape(GROUP, 16, 128)
-    for device in range(GROUP):
-        low = 128 * (device // 8)
-        values = pgrad[:, low : low + 128]
-        if device % 8:
-            values = pltpu.roll(values, 128 - 16 * (device % 8), axis=1)
-        part[device, 32:40, :] = values
-
-    for bits in mates:
-        other, device = mate(bits)
-        pltpu.make_async_remote_copy(
-            src_ref=part.at[other],
-            dst_ref=part_in.at[bits - 1],
-            send_sem=send_sem.at[3],
-            recv_sem=recv_sem.at[3],
-            device_id=device,
-            device_id_type=MESH,
-        ).start()
 
     stores = [
         pltpu.make_async_copy(source, target, store_sem.at[at])

time: 49.1 us -> 46.8 us (0.953)
  Pallas kernels: 48.3 us -> 46 us
    pallas_call x1, Pallas kernels: 46.7 us -> 44.3 us  [local(): pl.pallas_call(kernel, out_shape=results, in_specs=[far] * 11, out_specs=...]
where the time goes in v3:
time: 46.8 us; the launch traced here: 46.6 us
  Pallas kernels  46 us (98%)
  between operations  0.64 us (1%)
    pallas_call x1, Pallas kernels, local(): pl.pallas_call(kernel, out_shape=results, in_specs=[far] * 11, out_specs=...  44.3 us
    pallas_call x1, Pallas kernels, local(): pl.pallas_call(settle, out_shape=results, in_specs=[far] * 4, out_specs=(...  1.61 us

profile of v3, /device:TPU:1, one launch (start us, length us, event | category | flops | bytes accessed | tf_op | source)
XLA Modules:
  0.0 46.6 jit_solution(1359964312770986428)
XLA Ops:
  0.6 44.3 %shard_map.138 = (bf16[25,16,128]{2,1,0:T(8,128)(2,1)}, f32[16,128]{1,0:T(8,128)}, f32[16,128]{1,0:T(8,128)}, f32[3,1,16]{2,1,0:T(1,128)}) custom-call(bf16[25,16,128]{2,1,0:T(8,128)(2,1)} %bitcast.17, f32[3,1,16]{2,1,0:T(1,128)} %bitcast.22, s32[1,8]{1,0:T(1,128)} %bitcast.23, s32[16,32]{1,0:T(8,128)} %bitcast.19, f32[3,1,512]{2,1,0:T(1,128)} %bitcast.21, ...), custom_call_target="tpu_custom_call" | custom-call | tf_op jit(solution)/shard_map/pallas_call | solution.py:536
  45.0 1.6 %shard_map.139 = (bf16[25,16,128]{2,1,0:T(8,128)(2,1)}, f32[16,128]{1,0:T(8,128)}, f32[16,128]{1,0:T(8,128)}, f32[3,1,16]{2,1,0:T(1,128)}) custom-call(bf16[25,16,128]{2,1,0:T(8,128)(2,1)} %get-tuple-element.12.refs_0_, f32[16,128]{1,0:T(8,128)} %get-tuple-element.13.refs_1_, f32[16,128]{1,0:T(8,128)} %get-tuple-element.14.refs_2_, ...), custom_call_target="tpu_custom_call" | custom-call | tf_op jit(solution)/shard_map/pallas_call | solution.py:591

commit v4 on v3

--- a/solution.py
+++ b/solution.py
@@ -21,6 +21,7 @@
 GROUP = 16
 PEERS = 32
 CENTER = 13
+SENT = 35
 ROWS = 10
 
 half_zero = (0, 2, 6, 12, 20, 3, 7, 13, 21)
@@ -29,7 +30,8 @@
 
 
 x_hops, y_hops = (0, 1, 2, 1), (0, 4, 1, 3, 2, 2, 2, 2)
-mates = sorted(range(1, GROUP), key=lambda bits: -(x_hops[bits >> 2] + (bits >> 1) % 2))
+SIBLING = 8
+mates = sorted(range(1, SIBLING), key=lambda bits: -(x_hops[bits >> 1] + bits % 2))
 fellows = sorted(
     range(1, PEERS), key=lambda bits: -(y_hops[bits % 8] + (0, 2, 4, 2)[bits >> 3])
 )
@@ -104,6 +106,8 @@
     tiles_in,
     summed,
     part,
+    pair_in,
+    merged,
     part_in,
     load_sem,
     store_sem,
@@ -116,14 +120,15 @@
     ring_sem,
 ):
     px, py, pz = lax.axis_index("gx"), lax.axis_index("gy"), lax.axis_index("gz")
-    group = (pz // 2) * 4 + (px % 2) * 2 + py % 2
+    core = py % 2
+    group = core * 8 + (pz // 2) * 2 + px % 2
     peer = (px // 2) * 8 + (py // 2) * 2 + pz % 2
 
     def turns_of(p):
         return 1 - 2 * (p % 2), 2 - 4 * ((p // 2) % 2), 4 - 8 * (p // 4)
 
     x_turns, y_turns, z_turns = turns_of(px), turns_of(py), turns_of(pz)
-    group_turns = (y_turns[0], 2 * x_turns[0], 2 * z_turns[1], 2 * z_turns[2])
+    group_turns = (x_turns[0], z_turns[1], z_turns[2], 8 * y_turns[0])
     peer_turns = (z_turns[0], y_turns[1], y_turns[2], 4 * x_turns[1], 4 * x_turns[2])
 
     def turned(start, bits, steps):
@@ -134,9 +139,9 @@
 
     def mate(bits):
         return turned(group, bits, group_turns), (
-            turned(px, bits >> 1 & 1, x_turns),
-            turned(py, bits & 1, y_turns),
-            turned(pz, (bits >> 2) << 1, z_turns),
+            turned(px, bits & 1, x_turns),
+            turned(py, bits >> 3, y_turns),
+            turned(pz, (bits >> 1 & 3) << 1, z_turns),
         )
 
     def fellow(bits):
@@ -185,26 +190,25 @@
         greet(fellow(bits)[1])
     for device in around_z + around_y + around_x:
         greet(device)
-    for bits in mates:
+    for bits in mates + [SIBLING]:
         greet(mate(bits)[1])
 
     for load in loads[:3]:
         load.wait()
     atoms[group, 0:16, :] = first_ref[...].astype(F32)
     atoms[group, 16:32, :] = cot_ref[...]
-    atoms[group, 32:40, :] = jnp.zeros((8, 128), F32)
+    trip[...] = jnp.zeros((8, 128), F32)
     for axis, index in enumerate((px, py, pz)):
         corner = cell_length * index.astype(F32)
-        atoms[group, 32 + axis : 33 + axis, 0:16] = (pos_ref[axis] + corner) / (
-            cell_length * side
-        )
-
-    pl.semaphore_wait(barrier, len(mates) + len(along_ring) + len(across_rings) + 6)
+        trip[axis : axis + 1, 0:16] = (pos_ref[axis] + corner) / (cell_length * side)
+    atoms[group, 32:40, :] = pltpu.roll(trip[...], 16 * (group % 8), axis=1)
+
+    pl.semaphore_wait(barrier, len(mates) + 1 + len(along_ring) + len(across_rings) + 6)
 
     for bits in mates:
         pltpu.make_async_remote_copy(
-            src_ref=atoms.at[group],
-            dst_ref=atoms.at[group],
+            src_ref=atoms.at[group, pl.ds(0, SENT)],
+            dst_ref=atoms.at[group, pl.ds(0, SENT)],
             send_sem=send_sem.at[0],
             recv_sem=recv_sem.at[0],
             device_id=mate(bits)[1],
@@ -324,16 +328,22 @@
         mixers.extend(split(values))
     mixers = jnp.concatenate(mixers, axis=0)
 
-    wait_bytes(atoms.at[pl.ds(0, GROUP - 1)], recv_sem.at[0])
+    wait_bytes(atoms.at[pl.ds(0, 7), pl.ds(0, SENT)], recv_sem.at[0])
+    ours = pl.ds(core * 8, 8)
+    pltpu.make_async_remote_copy(
+        src_ref=atoms.at[ours, pl.ds(0, SENT)],
+        dst_ref=atoms.at[ours, pl.ds(0, SENT)],
+        send_sem=send_sem.at[4],
+        recv_sem=recv_sem.at[4],
+        device_id=mate(SIBLING)[1],
+        device_id_type=MESH,
+    ).start()
+    wait_bytes(atoms.at[pl.ds(0, 8), pl.ds(0, SENT)], recv_sem.at[4])
     charges = atoms[:, 0:16, :].reshape(256, 128)
     grad_input = atoms[:, 16:32, :].reshape(256, 128)
-    places = []
-    for low in (0, 8):
-        total = atoms[low, 32:40, :]
-        for step in range(1, 8):
-            total = total + pltpu.roll(atoms[low + step, 32:40, :], 16 * step, axis=1)
-        places.append(total)
-    places = jnp.concatenate(places, axis=1)
+    places = jnp.concatenate(
+        [jnp.sum(atoms[low : low + 8, 32:35, :], axis=0) for low in (0, 8)], axis=1
+    )
     turns = (
         triples_down[:, 0:1] * places[0:1, :]
         + triples_down[:, 1:2] * places[1:2, :]
@@ -428,11 +438,23 @@
             values = pltpu.roll(values, 128 - 16 * (device % 8), axis=1)
         part[device, 32:40, :] = values
 
+    theirs = pl.ds(8 - core * 8, 8)
+    pltpu.make_async_remote_copy(
+        src_ref=part.at[theirs, pl.ds(0, SENT)],
+        dst_ref=pair_in.at[:, pl.ds(0, SENT)],
+        send_sem=send_sem.at[5],
+        recv_sem=recv_sem.at[5],
+        device_id=mate(SIBLING)[1],
+        device_id_type=MESH,
+    ).start()
+    wait_bytes(pair_in.at[:, pl.ds(0, SENT)], recv_sem.at[5])
+    merged[:, 0:SENT, :] = part[ours, 0:SENT, :] + pair_in[:, 0:SENT, :]
+    own = group % 8
     for bits in mates:
         other, device = mate(bits)
         pltpu.make_async_remote_copy(
-            src_ref=part.at[other],
-            dst_ref=part_in.at[bits - 1],
+            src_ref=merged.at[other % 8, pl.ds(0, SENT)],
+            dst_ref=part_in.at[bits - 1, pl.ds(0, SENT)],
             send_sem=send_sem.at[3],
             recv_sem=recv_sem.at[3],
             device_id=device,
@@ -483,19 +505,22 @@
     ]
     stores[0].start()
 
-    wait_bytes(part_in, recv_sem.at[3])
-    result = part[group] + jnp.sum(part_in[...], axis=0)
-    result_ref[...] = result
+    all_parts = part_in.at[:, pl.ds(0, SENT), :]
+    wait_bytes(all_parts, recv_sem.at[3])
+    result = merged[own, 0:SENT, :] + jnp.sum(part_in[:, 0:SENT, :], axis=0)
+    result_ref[0:32] = result[0:32]
     for axis in range(3):
         pgrad_ref[axis] = result[32 + axis : 33 + axis, 0:16]
     for store in stores[1:]:
         store.start()
 
     wait_bytes(table.at[pl.ds(0, 26)], halo_send)
-    wait_bytes(part_in, send_sem.at[0])
+    wait_bytes(all_parts, send_sem.at[0])
+    wait_bytes(pair_in.at[:, pl.ds(0, SENT)], send_sem.at[4])
     wait_bytes(all_tiles, send_sem.at[1])
     wait_bytes(summed.at[pl.ds(0, PEERS - 1)], send_sem.at[2])
-    wait_bytes(part_in, send_sem.at[3])
+    wait_bytes(all_parts, send_sem.at[3])
+    wait_bytes(pair_in.at[:, pl.ds(0, SENT)], send_sem.at[5])
     for store in stores:
         store.wait()
 
@@ -561,15 +586,17 @@
             pltpu.VMEM((PEERS - 1, 16, 128), F32),
             pltpu.VMEM((PEERS, 8, 128), F32),
             pltpu.VMEM((GROUP, 40, 128), F32),
-            pltpu.VMEM((GROUP - 1, 40, 128), F32),
+            pltpu.VMEM((8, 40, 128), F32),
+            pltpu.VMEM((8, 40, 128), F32),
+            pltpu.VMEM((7, 40, 128), F32),
             pltpu.SemaphoreType.DMA((12,)),
             pltpu.SemaphoreType.DMA((4,)),
             pltpu.SemaphoreType.DMA,
             pltpu.SemaphoreType.DMA((2,)),
             pltpu.SemaphoreType.DMA((2,)),
             pltpu.SemaphoreType.DMA((2,)),
-            pltpu.SemaphoreType.DMA((4,)),
-            pltpu.SemaphoreType.DMA((4,)),
+            pltpu.SemaphoreType.DMA((6,)),
+            pltpu.SemaphoreType.DMA((6,)),
             pltpu.SemaphoreType.REGULAR,
         ],
         compiler_params=pltpu.CompilerParams(

time: 46.8 us -> 45 us (0.962)
  Pallas kernels: 46 us -> 44.2 us
    pallas_call x1, Pallas kernels: 44.3 us -> 42.6 us  [local(): pl.pallas_call(kernel, out_shape=results, in_specs=[far] * 11, out_specs=...]
where the time goes in v4:
time: 45 us; the launch traced here: 44.9 us
  Pallas kernels  44.2 us (98%)
  between operations  0.64 us (1%)
    pallas_call x1, Pallas kernels, local(): pl.pallas_call(kernel, out_shape=results, in_specs=[far] * 11, out_specs=...  42.6 us
    pallas_call x1, Pallas kernels, local(): pl.pallas_call(settle, out_shape=results, in_specs=[far] * 4, out_specs=(...  1.61 us

profile of v4, /device:TPU:1, one launch (start us, length us, event | category | flops | bytes accessed | tf_op | source)
XLA Modules:
  0.0 44.9 jit_solution(3909028452907807145)
XLA Ops:
  0.6 42.6 %shard_map.138 = (bf16[25,16,128]{2,1,0:T(8,128)(2,1)}, f32[16,128]{1,0:T(8,128)}, f32[16,128]{1,0:T(8,128)}, f32[3,1,16]{2,1,0:T(1,128)}) custom-call(bf16[25,16,128]{2,1,0:T(8,128)(2,1)} %bitcast.17, f32[3,1,16]{2,1,0:T(1,128)} %bitcast.22, s32[1,8]{1,0:T(1,128)} %bitcast.23, s32[16,32]{1,0:T(8,128)} %bitcast.19, f32[3,1,512]{2,1,0:T(1,128)} %bitcast.21, ...), custom_call_target="tpu_custom_call" | custom-call | tf_op jit(solution)/shard_map/pallas_call | solution.py:561
  43.2 1.6 %shard_map.139 = (bf16[25,16,128]{2,1,0:T(8,128)(2,1)}, f32[16,128]{1,0:T(8,128)}, f32[16,128]{1,0:T(8,128)}, f32[3,1,16]{2,1,0:T(1,128)}) custom-call(bf16[25,16,128]{2,1,0:T(8,128)(2,1)} %get-tuple-element.12.refs_0_, f32[16,128]{1,0:T(8,128)} %get-tuple-element.13.refs_1_, f32[16,128]{1,0:T(8,128)} %get-tuple-element.14.refs_2_, ...), custom_call_target="tpu_custom_call" | custom-call | tf_op jit(solution)/shard_map/pallas_call | solution.py:618

commit v5 on v4

--- a/solution.py
+++ b/solution.py
@@ -48,9 +48,9 @@
     return lax.dot_general(a, b, (dims, ((), ())), preferred_element_type=F32)
 
 
-def dot3(a, b, dims=((1,), (0,))):
-    a_high, a_low = split(a)
-    b_high, b_low = split(b)
+def dot3(a_split, b_split, dims=((1,), (0,))):
+    a_high, a_low = a_split
+    b_high, b_low = b_split
     return dot(a_high, b_high, dims) + (dot(a_high, b_low, dims) + dot(a_low, b_high, dims))
 
 
@@ -408,29 +408,45 @@
 
     scale = 1.0 / math.sqrt(atoms_total * wave_vectors)
     loads[8].wait()
-    wait_bytes(summed.at[pl.ds(0, PEERS - 1)], recv_sem.at[2])
+    factor = filt[...] * scale
+    factor = jnp.concatenate([factor, factor], axis=0)
     mean_charge = total_charge / atoms_total
     plane_down = jnp.broadcast_to(plane, (8, 128)).T[:, 0:1]
-    factor = filt[...] * scale
-    factor = jnp.concatenate([factor, factor], axis=0)
+    across_split = split(waves_across)
+    around_split = split(waves_across - plane / atoms_total)
+    sides = split(jnp.concatenate([grad_input, charges - mean_charge], axis=1))
+    wait_bytes(summed.at[pl.ds(0, PEERS - 1)], recv_sem.at[2])
     filtered = factor * (summed[0:16].reshape(128, 128) - plane_down * mean_charge)
     filtered_response = factor * summed[16:32].reshape(128, 128)
-    long_part = dot3(waves_across, filtered)
-    charge_part = dot3(waves_across - plane / atoms_total, filtered_response)
+    long_part = dot3(across_split, split(filtered))
+    charge_part = dot3(around_split, split(filtered_response))
+
+    part[:, 0:16, :] = long_part.reshape(GROUP, 16, 128)
+    part[:, 16:32, :] = charge_part.reshape(GROUP, 16, 128)
+    theirs = pl.ds(8 - core * 8, 8)
+
+    def pair_up(first, count):
+        pltpu.make_async_remote_copy(
+            src_ref=part.at[theirs, pl.ds(first, count)],
+            dst_ref=pair_in.at[:, pl.ds(first, count)],
+            send_sem=send_sem.at[5],
+            recv_sem=recv_sem.at[5],
+            device_id=mate(SIBLING)[1],
+            device_id_type=MESH,
+        ).start()
+
+    pair_up(0, 32)
 
     def swapped(values):
         return jnp.concatenate([values[64:], values[:64]], axis=0)
 
     both = jnp.concatenate([swapped(filtered), swapped(filtered_response)], axis=1)
-    sides = jnp.concatenate([grad_input, charges - mean_charge], axis=1)
-    phase_grad = waves * dot3(both, sides, ((1,), (1,)))
+    phase_grad = waves * dot3(split(both), sides, ((1,), (1,)))
     signed = jnp.where(iota((8, 128), 1) < 64, triples, -triples).astype(BF16)
     phase_high, phase_low = split(phase_grad)
     pgrad = (dot(signed, phase_high) + dot(signed, phase_low)) * (
         2.0 * math.pi / (cell_length * side)
     )
-    part[:, 0:16, :] = long_part.reshape(GROUP, 16, 128)
-    part[:, 16:32, :] = charge_part.reshape(GROUP, 16, 128)
     for device in range(GROUP):
         low = 128 * (device // 8)
         values = pgrad[:, low : low + 128]
@@ -438,15 +454,7 @@
             values = pltpu.roll(values, 128 - 16 * (device % 8), axis=1)
         part[device, 32:40, :] = values
 
-    theirs = pl.ds(8 - core * 8, 8)
-    pltpu.make_async_remote_copy(
-        src_ref=part.at[theirs, pl.ds(0, SENT)],
-        dst_ref=pair_in.at[:, pl.ds(0, SENT)],
-        send_sem=send_sem.at[5],
-        recv_sem=recv_sem.at[5],
-        device_id=mate(SIBLING)[1],
-        device_id_type=MESH,
-    ).start()
+    pair_up(32, SENT - 32)
     wait_bytes(pair_in.at[:, pl.ds(0, SENT)], recv_sem.at[5])
     merged[:, 0:SENT, :] = part[ours, 0:SENT, :] + pair_in[:, 0:SENT, :]
     own = group % 8
@@ -527,8 +535,15 @@
 
 def settle(*refs):
     sources, targets, held, sems = refs[0:4], refs[4:8], refs[8:12], refs[12]
-    into = [pltpu.make_async_copy(sources[at], held[at], sems.at[at]) for at in range(4)]
-    out = [pltpu.make_async_copy(held[at], targets[at], sems.at[4 + at]) for at in range(4)]
+    pieces = [(0, pl.ds(5 * at, 5)) for at in range(5)] + [(at, slice(None)) for at in (1, 2, 3)]
+    into = [
+        pltpu.make_async_copy(sources[of].at[rows], held[of].at[rows], sems.at[at])
+        for at, (of, rows) in enumerate(pieces)
+    ]
+    out = [
+        pltpu.make_async_copy(held[of].at[rows], targets[of].at[rows], sems.at[8 + at])
+        for at, (of, rows) in enumerate(pieces)
+    ]
     for copy in into:
         copy.start()
     for arrive, leave in zip(into, out):
@@ -621,7 +636,7 @@
         in_specs=[far] * 4,
         out_specs=(far,) * 4,
         scratch_shapes=[pltpu.VMEM(held_one.shape, held_one.dtype) for held_one in results]
-        + [pltpu.SemaphoreType.DMA((8,))],
+        + [pltpu.SemaphoreType.DMA((16,))],
         compiler_params=pltpu.CompilerParams(vmem_limit_bytes=60 * 1024 * 1024),
     )(*held)
     return (

time: 45 us -> 45 us (level)
  no operation moved by 1% of the time
where the time goes in v5:
time: 45 us; the launch traced here: 44.8 us
  Pallas kernels  44.1 us (98%)
  between operations  0.64 us (1%)
    pallas_call x1, Pallas kernels, local(): pl.pallas_call(kernel, out_shape=results, in_specs=[far] * 11, out_specs=...  42.6 us
    pallas_call x1, Pallas kernels, local(): pl.pallas_call(settle, out_shape=results, in_specs=[far] * 4, out_specs=(...  1.55 us

profile of v5, /device:TPU:1, one launch (start us, length us, event | category | flops | bytes accessed | tf_op | source)
XLA Modules:
  0.0 44.8 jit_solution(12754875374858541823)
XLA Ops:
  0.6 42.6 %shard_map.138 = (bf16[25,16,128]{2,1,0:T(8,128)(2,1)}, f32[16,128]{1,0:T(8,128)}, f32[16,128]{1,0:T(8,128)}, f32[3,1,16]{2,1,0:T(1,128)}) custom-call(bf16[25,16,128]{2,1,0:T(8,128)(2,1)} %bitcast.17, f32[3,1,16]{2,1,0:T(1,128)} %bitcast.22, s32[1,8]{1,0:T(1,128)} %bitcast.23, s32[16,32]{1,0:T(8,128)} %bitcast.19, f32[3,1,512]{2,1,0:T(1,128)} %bitcast.21, ...), custom_call_target="tpu_custom_call" | custom-call | tf_op jit(solution)/shard_map/pallas_call | solution.py:576
  43.2 1.6 %shard_map.139 = (bf16[25,16,128]{2,1,0:T(8,128)(2,1)}, f32[16,128]{1,0:T(8,128)}, f32[16,128]{1,0:T(8,128)}, f32[3,1,16]{2,1,0:T(1,128)}) custom-call(bf16[25,16,128]{2,1,0:T(8,128)(2,1)} %get-tuple-element.12.refs_0_, f32[16,128]{1,0:T(8,128)} %get-tuple-element.13.refs_1_, f32[16,128]{1,0:T(8,128)} %get-tuple-element.14.refs_2_, ...), custom_call_target="tpu_custom_call" | custom-call | tf_op jit(solution)/shard_map/pallas_call | solution.py:633
